TPU v7x, 32 devices: a whole 2x2x4 slice. The times are simulated.
32 devices in a mesh: expert: 8 (over z, y), tensor: 4 (over x, core).
Axes of the slice: x: 2, y: 2, z: 4, core: 2. Of those that a mesh axis runs over, the one named last changes fastest.
Arguments:
- tokens: bfloat16 [7880, 512], P('expert'), may hold values from -6 to 6
- routes: int32 [2, 7880, 2], P(None, 'expert'), may hold values from 0 to 7, all different within a row
- ln_gain: float32 [2, 2, 512], replicated, may hold values from 0.5 to 1.5
- ln_bias: float32 [2, 2, 512], replicated, may hold values from -1.5 to 1.5
- w_qkv: bfloat16 [2, 3, 512, 512], P(None, None, None, 'tensor'), may hold values from -0.25 to 0.25
- w_out: bfloat16 [2, 512, 512], P(None, 'tensor'), may hold values from -1 to 1
- w_router: bfloat16 [2, 512, 8], replicated, may hold values from -0.1875 to 0.1875
- w_up: bfloat16 [2, 8, 512, 2048], P(None, 'expert', None, 'tensor'), may hold values from -0.25 to 0.25
- w_down: bfloat16 [2, 8, 2048, 512], P(None, 'expert', 'tensor'), may hold values from -0.1875 to 0.1875
- cotangent: bfloat16 [7880, 512], P('expert'), may hold values from -6 to 6
Outputs:
- result: bfloat16 [7880, 512], P('expert')
- grad_tokens: float32 [7880, 512], P('expert')
- grad_gain: float32 [2, 2, 512], replicated
- grad_bias_one: float32 [2, 512], replicated
- grad_bias_two: float32 [2, 512], replicated
- grad_qkv: float32 [2, 3, 512, 512], P(None, None, None, 'tensor')
- grad_out: float32 [2, 512, 512], P(None, 'tensor')
- grad_router: float32 [2, 512, 8], replicated
- grad_up: float32 [2, 8, 512, 2048], P(None, 'expert', None, 'tensor')
- grad_down: float32 [2, 8, 2048, 512], P(None, 'expert', 'tensor')
Inputs may be any that keep to these rules, and one draw needn't show every extreme that they name: `routes`: each token names 2 different experts in each block; every expert is named by some token.
All inputs are finite; a program needn't handle non-finite values.
Results may differ from a plain program's by a relative error of at most 0.034.
Values may be sent and summed in bfloat16 or wider, within the bound.
A program may use at most 128 MiB of HBM per device.

v0:
```python
import jax
import jax.numpy as jnp
from jax import lax
from jax.sharding import PartitionSpec as P

HEAD_DIM = 64
SEQ = 197
LAYERS = 2


EPS = 1e-06


def norm_forward(stream, gain_row, bias_row):
    centered = stream - jnp.mean(stream, -1, keepdims=True)
    scaled = lax.rsqrt(jnp.mean(centered * centered, -1, keepdims=True) + EPS)
    normed = centered * scaled
    return (normed * gain_row + bias_row, normed, scaled)


def norm_backward(grad_in, normed, scaled, gain_row):
    grad_normed = grad_in * gain_row
    inner = (
        grad_normed
        - jnp.mean(grad_normed, -1, keepdims=True)
        - normed * jnp.mean(grad_normed * normed, -1, keepdims=True)
    )
    return (inner * scaled, jnp.sum(grad_in * normed, 0), jnp.sum(grad_in, 0))


def assign_slots(route_pair, experts, capacity):
    flat_route = route_pair.reshape(-1)
    onehot = (flat_route[:, None] == jnp.arange(experts, dtype=jnp.int32)[None, :]).astype(
        jnp.int32
    )
    before = jnp.cumsum(onehot, 0) - onehot
    place_in = jnp.sum(before * onehot, 1)
    kept_mask = place_in < capacity
    slot_total = experts * capacity
    slot_code = jnp.where(kept_mask, place_in * experts + flat_route, slot_total)
    member = jnp.arange(flat_route.shape[0], dtype=jnp.int32)
    slot_member = jnp.zeros((slot_total,), jnp.int32).at[slot_code].set(member, mode="drop")
    filled = jnp.zeros((slot_total,), jnp.bool_).at[slot_code].set(True, mode="drop")
    return (
        slot_code.reshape(route_pair.shape),
        kept_mask.reshape(route_pair.shape),
        slot_member,
        filled,
    )


def to_experts(slot_rows):
    return lax.all_to_all(slot_rows, "expert", split_axis=1, concat_axis=1, tiled=True)


def return_rows(left_rows, right_mat, contract, capacity, experts):
    per_rank = capacity // lax.axis_size("tensor")
    product = lax.dot_general(
        left_rows, right_mat, (((1,), (contract,)), ((), ())), preferred_element_type=jnp.float32
    )
    share_rows = lax.psum_scatter(
        product.reshape(per_rank * lax.axis_size("tensor"), experts, product.shape[-1]).astype(
            jnp.bfloat16
        ),
        "tensor",
        scatter_dimension=0,
        tiled=True,
    )
    whole_rows = lax.all_gather(share_rows, "tensor", axis=0, tiled=True)
    back_rows = lax.all_to_all(whole_rows, "expert", split_axis=1, concat_axis=1, tiled=True)
    return back_rows.reshape(capacity * experts, -1)


def layer_forward(stream, route_pair, gain_pair, bias_pair, w_qkv, w_out, w_router, w_up, w_down):
    tok_rows = stream.shape[0]
    images = tok_rows // SEQ
    experts = w_router.shape[1]
    tensor_size = lax.axis_size("tensor")
    capacity = tensor_size * max(1, 10 * tok_rows // (4 * experts * tensor_size))
    scale_factor = HEAD_DIM ** (-0.5)
    normed_in, normed1, scaled1 = norm_forward(stream, gain_pair[0], bias_pair[0])
    hidden_in = normed_in.astype(jnp.bfloat16)
    proj = jnp.einsum("rd,cdf->crf", hidden_in, w_qkv, preferred_element_type=jnp.float32).astype(
        jnp.bfloat16
    )
    query = proj[0].reshape(images, SEQ, -1, HEAD_DIM)
    keyed = proj[1].reshape(images, SEQ, -1, HEAD_DIM)
    valued = proj[2].reshape(images, SEQ, -1, HEAD_DIM)
    scores = (
        jnp.einsum("bqhe,bkhe->bhqk", query, keyed, preferred_element_type=jnp.float32)
        * scale_factor
    )
    expd = jnp.exp(scores - jnp.max(scores, -1, keepdims=True))
    attn_prob = expd / jnp.sum(expd, -1, keepdims=True)
    prob_low = attn_prob.astype(jnp.bfloat16)
    mixed_heads = (
        jnp.einsum("bhqk,bkhe->bqhe", prob_low, valued, preferred_element_type=jnp.float32)
        .reshape(tok_rows, -1)
        .astype(jnp.bfloat16)
    )
    attn_part = jnp.dot(mixed_heads, w_out, preferred_element_type=jnp.float32)
    attn_out = lax.psum(attn_part.astype(jnp.bfloat16), "tensor").astype(jnp.float32)
    after_attn = stream + attn_out
    normed_two, normed2, scaled2 = norm_forward(after_attn, gain_pair[1], bias_pair[1])
    hidden_two = normed_two.astype(jnp.bfloat16)
    logits = jnp.dot(hidden_two, w_router, preferred_element_type=jnp.float32)
    chosen = jnp.take_along_axis(logits, route_pair, 1)
    shifted = jnp.exp(chosen - jnp.max(chosen, -1, keepdims=True))
    gate_share = shifted / jnp.sum(shifted, -1, keepdims=True)
    slot_code, kept_mask, slot_member, filled = assign_slots(route_pair, experts, capacity)
    send_rows = jnp.where(
        filled[:, None], jnp.take(hidden_two, slot_member // 2, 0), jnp.zeros((), jnp.bfloat16)
    )
    recv_rows = to_experts(send_rows.reshape(capacity, experts, -1)).reshape(capacity * experts, -1)
    up_local = w_up[0]
    down_local = w_down[0]
    pre_act = jnp.dot(recv_rows, up_local, preferred_element_type=jnp.float32)
    hidden = jax.nn.gelu(pre_act).astype(jnp.bfloat16)
    back_rows = return_rows(hidden, down_local, 0, capacity, experts)
    safe_code = jnp.minimum(slot_code, capacity * experts - 1)
    picked = jnp.take(back_rows, safe_code, 0).astype(jnp.float32) * kept_mask[..., None].astype(
        jnp.float32
    )
    next_stream = after_attn + jnp.sum(gate_share[..., None] * picked, 1)
    saved = {
        "normed1": normed1,
        "scaled1": scaled1,
        "hidden_in": hidden_in,
        "query": query,
        "keyed": keyed,
        "valued": valued,
        "attn_prob": attn_prob,
        "prob_low": prob_low,
        "mixed_heads": mixed_heads,
        "normed2": normed2,
        "scaled2": scaled2,
        "hidden_two": hidden_two,
        "gate_share": gate_share,
        "safe_code": safe_code,
        "kept_mask": kept_mask,
        "slot_member": slot_member,
        "filled": filled,
        "recv_rows": recv_rows,
        "pre_act": pre_act,
        "hidden": hidden,
        "picked": picked,
    }
    return (next_stream, saved)


def layer_backward(grad_stream, route_pair, gain_pair, w_qkv, w_out, w_router, w_up, w_down, saved):
    tok_rows = grad_stream.shape[0]
    images = tok_rows // SEQ
    experts = w_router.shape[1]
    tensor_size = lax.axis_size("tensor")
    capacity = tensor_size * max(1, 10 * tok_rows // (4 * experts * tensor_size))
    scale_factor = HEAD_DIM ** (-0.5)
    gate_share = saved["gate_share"]
    kept_mask = saved["kept_mask"].astype(jnp.float32)
    gate_grad = jnp.sum(grad_stream[:, None, :] * saved["picked"], -1)
    chosen_grad = gate_share * (gate_grad - jnp.sum(gate_share * gate_grad, -1, keepdims=True))
    expert_ids = jnp.arange(experts, dtype=jnp.int32)
    logit_grad = jnp.sum(
        chosen_grad[:, :, None]
        * (route_pair[:, :, None] == expert_ids[None, None, :]).astype(jnp.float32),
        1,
    ).astype(jnp.bfloat16)
    grad_router = jnp.einsum(
        "rd,re->de", saved["hidden_two"], logit_grad, preferred_element_type=jnp.float32
    )
    grad_two = jnp.einsum("re,de->rd", logit_grad, w_router, preferred_element_type=jnp.float32)
    slot_member = saved["slot_member"]
    slot_gate = jnp.take(gate_share.reshape(-1), slot_member, 0)
    slot_grad = jnp.take(grad_stream, slot_member // 2, 0) * slot_gate[:, None]
    out_grad = jnp.where(saved["filled"][:, None], slot_grad, 0.0).astype(jnp.bfloat16)
    recv_grad = to_experts(out_grad.reshape(capacity, experts, -1)).reshape(capacity * experts, -1)
    up_local = w_up[0]
    down_local = w_down[0]
    hidden_grad = jnp.einsum("sd,fd->sf", recv_grad, down_local, preferred_element_type=jnp.float32)
    grad_down = jnp.einsum(
        "sf,sd->fd", saved["hidden"], recv_grad, preferred_element_type=jnp.float32
    )
    gelu_value, gelu_pull = jax.vjp(jax.nn.gelu, saved["pre_act"])
    pre_grad = gelu_pull(hidden_grad)[0].astype(jnp.bfloat16)
    grad_up = jnp.einsum(
        "sd,sf->df", saved["recv_rows"], pre_grad, preferred_element_type=jnp.float32
    )
    send_grad = return_rows(pre_grad, up_local, 1, capacity, experts)
    routed_back = (
        jnp.take(send_grad, saved["safe_code"], 0).astype(jnp.float32) * kept_mask[..., None]
    )
    grad_two = grad_two + jnp.sum(routed_back, 1)
    norm_two_grad, gain_two, bias_two = norm_backward(
        grad_two, saved["normed2"], saved["scaled2"], gain_pair[1]
    )
    grad_after = grad_stream + norm_two_grad
    out_low = grad_after.astype(jnp.bfloat16)
    grad_out = jnp.einsum(
        "rc,rd->cd", saved["mixed_heads"], out_low, preferred_element_type=jnp.float32
    )
    mixed_grad = jnp.einsum("rd,cd->rc", out_low, w_out, preferred_element_type=jnp.float32).astype(
        jnp.bfloat16
    )
    mixed_grad = mixed_grad.reshape(images, SEQ, -1, HEAD_DIM)
    attn_prob = saved["attn_prob"]
    value_grad = jnp.einsum(
        "bhqk,bqhe->bkhe", saved["prob_low"], mixed_grad, preferred_element_type=jnp.float32
    )
    prob_grad = jnp.einsum(
        "bqhe,bkhe->bhqk", mixed_grad, saved["valued"], preferred_element_type=jnp.float32
    )
    score_grad = (
        attn_prob * (prob_grad - jnp.sum(prob_grad * attn_prob, -1, keepdims=True))
    ).astype(jnp.bfloat16)
    query_grad = (
        jnp.einsum(
            "bhqk,bkhe->bqhe", score_grad, saved["keyed"], preferred_element_type=jnp.float32
        )
        * scale_factor
    )
    key_grad = (
        jnp.einsum(
            "bhqk,bqhe->bkhe", score_grad, saved["query"], preferred_element_type=jnp.float32
        )
        * scale_factor
    )
    proj_grad = (
        jnp.stack([query_grad, key_grad, value_grad]).reshape(3, tok_rows, -1).astype(jnp.bfloat16)
    )
    grad_qkv = jnp.einsum(
        "rd,crf->cdf", saved["hidden_in"], proj_grad, preferred_element_type=jnp.float32
    )
    input_part = jnp.einsum("crf,cdf->rd", proj_grad, w_qkv, preferred_element_type=jnp.float32)
    input_grad = lax.psum(input_part.astype(jnp.bfloat16), "tensor").astype(jnp.float32)
    norm_one_grad, gain_one, bias_one = norm_backward(
        input_grad, saved["normed1"], saved["scaled1"], gain_pair[0]
    )
    grad_input = grad_after + norm_one_grad
    gains_grad = jnp.stack([gain_one, gain_two])
    biases_grad = jnp.stack([bias_one, bias_two])
    return (
        grad_input,
        (gains_grad, biases_grad, grad_qkv, grad_out, grad_router, grad_up, grad_down),
    )


def body(tokens, routes, ln_gain, ln_bias, w_qkv, w_out, w_router, w_up, w_down, cotangent):

    def run_layer(stream, layer_index):
        return layer_forward(
            stream,
            routes[layer_index],
            ln_gain[layer_index],
            ln_bias[layer_index],
            w_qkv[layer_index],
            w_out[layer_index],
            w_router[layer_index],
            w_up[layer_index],
            w_down[layer_index],
        )

    stream = tokens.astype(jnp.float32)
    inputs = []
    stored = []
    for layer_index in range(LAYERS):
        inputs.append(stream)
        stream, saved = run_layer(stream, layer_index)
        stored.append(saved)
    result = stream.astype(jnp.bfloat16)
    grad_stream = cotangent.astype(jnp.float32)
    per_layer = [None] * LAYERS
    for layer_index in reversed(range(LAYERS)):
        unused_out, saved = run_layer(inputs[layer_index], layer_index)
        grad_stream, per_layer[layer_index] = layer_backward(
            grad_stream,
            routes[layer_index],
            ln_gain[layer_index],
            w_qkv[layer_index],
            w_out[layer_index],
            w_router[layer_index],
            w_up[layer_index],
            w_down[layer_index],
            saved,
        )
    stacked = [jnp.stack([entry[member] for entry in per_layer]) for member in range(7)]
    summed = lax.psum((stacked[0], stacked[1], stacked[2], stacked[3], stacked[4]), "expert")
    return (
        result,
        grad_stream,
        summed[0],
        summed[1][:, 0],
        summed[1][:, 1],
        summed[2],
        summed[3],
        summed[4],
        stacked[5][:, None],
        stacked[6][:, None],
    )


def solution(mesh):
    in_specs = (
        P("expert", None),
        P(None, "expert", None),
        P(),
        P(),
        P(None, None, None, "tensor"),
        P(None, "tensor", None),
        P(),
        P(None, "expert", None, "tensor"),
        P(None, "expert", "tensor", None),
        P("expert", None),
    )
    out_specs = (
        P("expert", None),
        P("expert", None),
        P(),
        P(),
        P(),
        P(None, None, None, "tensor"),
        P(None, "tensor", None),
        P(),
        P(None, "expert", None, "tensor"),
        P(None, "expert", "tensor", None),
    )
    return jax.shard_map(body, mesh=mesh, in_specs=in_specs, out_specs=out_specs, check_vma=False)
```

profile of v0, /device:TPU:0, one launch (start us, length us, event | category | flops | bytes accessed | tf_op | source)
XLA Modules:
  0.0 1235.1 jit_solution(18280467942668930918)
XLA Ops:
  28.7 10.1 scatter_custom_fusion.1
  38.9 11.2 scatter_custom_fusion
  50.2 12.8 %all-reduce.10.cloned.1.call-done = bf16[985,512]{1,0:T(8,128)(2,1)} async-done(((bf16[985,512]{1,0:T(8,128)(2,1)}), bf16[985,512]{1,0:T(8,128)(2,1)}) %all-reduce.10.cloned.1.call-update) | async-done | bytes 1008656 | tf_op jit(solution)/shard_map/psum | solution.py:102
  66.4 8.2 gather_fusion.1
  78.9 61.8 %all_to_all.44 = bf16[304,8,512]{2,0,1:T(8,128)(2,1)S(1)} all-to-all(bf16[304,8,512]{2,0,1:T(8,128)(2,1)S(1)} %copy.416), channel_id=1, replica_groups=mesh['expert'=8,'tensor'=4] {'expert'}, dimensions={1} | all-to-all | bytes 4980736 | tf_op jit(solution)/shard_map/all_to_all | solution.py:53
  149.4 32.5 %reduce-scatter.5.cloned.1.call-done = bf16[76,8,512]{2,1,0:T(8,128)(2,1)} async-done(((bf16[304,8,512]{2,1,0:T(8,128)(2,1)}), bf16[76,8,512]{2,1,0:T(8,128)(2,1)}) %reduce-scatter.5.cloned.1.call-update) | async-done | bytes 622608 | tf_op jit(solution)/shard_map/reduce_scatter | solution.py:61
  181.9 26.4 %all-gather.5.cloned.1.call-done = bf16[304,8,512]{2,1,0:T(8,128)(2,1)} async-done(((bf16[76,8,512]{2,1,0:T(8,128)(2,1)}), bf16[304,8,512]{2,1,0:T(8,128)(2,1)}) %all-gather.5.cloned.1.call-update) | async-done | bytes 2490384 | tf_op jit(solution)/shard_map/all_gather | solution.py:69
  212.3 5.5 all-to-all-start.1
  229.8 18.5 %gather_fusion = f32[1970]{0:T(1024)S(1)} fusion(f32[985,8]{0,1:T(8,128)S(1)} %fusion.187, s32[1970]{0:T(1024)S(1)} %reshape.568), kind=kCustom, calls=%fused_computation.clone | custom fusion | bytes 31520 | tf_op jit(solution)/shard_map/jit(take_along_axis)/gather | solution.py:107
  249.9 25.1 %all-to-all-done.1 = bf16[304,8,512]{2,0,1:T(8,128)(2,1)} async-done(((bf16[304,8,512]{2,0,1:T(8,128)(2,1)}), bf16[304,8,512]{2,0,1:T(8,128)(2,1)}, u32[]{:S(2)}, u32[]{:S(2)}) %all-to-all-start.1) | async-done | bytes 2490400 | tf_op jit(solution)/shard_map/all_to_all | solution.py:70
  278.1 9.2 gather_fusion.2
  292.8 21.4 %multiply_reduce_fusion.5 = f32[985,512]{1,0:T(8,128)S(1)} fusion(f32[985,2]{1,0:T(8,128)S(1)} %copy-done.32, f32[985,2]{1,0:T(8,128)S(1)} %copy.410, bf16[985,2,512]{2,1,0:T(2,128)(2,1)S(1)} %reshape.577, pred[985,2]{1,0:T(8,128)(4,1)S(1)} %copy-done.59), kind=kLoop, calls=%fused_computation.50 | loop fusion | flops 4538880 | bytes 4052290 | tf_op jit(solution)/shard_map/reduce_sum | solution.py:124
  328.5 11.4 scatter_custom_fusion.2
  339.9 10.0 scatter_custom_fusion.3
  349.9 12.6 %all-reduce.12.cloned.1.call-done = bf16[985,512]{1,0:T(8,128)(2,1)} async-done(((bf16[985,512]{1,0:T(8,128)(2,1)}), bf16[985,512]{1,0:T(8,128)(2,1)}) %all-reduce.12.cloned.1.call-update) | async-done | bytes 1008656 | tf_op jit(solution)/shard_map/psum | solution.py:102
  365.7 8.1 gather_fusion.4
  376.5 61.8 %all_to_all.45 = bf16[304,8,512]{2,0,1:T(8,128)(2,1)S(1)} all-to-all(bf16[304,8,512]{2,0,1:T(8,128)(2,1)S(1)} %copy.437), channel_id=1, replica_groups=mesh['expert'=8,'tensor'=4] {'expert'}, dimensions={1} | all-to-all | bytes 4980736 | tf_op jit(solution)/shard_map/all_to_all | solution.py:53
  449.5 7.5 gather_fusion.6
  458.0 18.5 %gather_fusion.3 = f32[1970]{0:T(1024)S(1)} fusion(f32[985,8]{0,1:T(8,128)S(1)} %fusion.184, s32[1970]{0:T(1024)S(1)} %reshape.579), kind=kCustom, calls=%fused_computation.5.clone | custom fusion | bytes 31520 | tf_op jit(solution)/shard_map/jit(take_along_axis)/gather | solution.py:107
  477.8 13.0 %gather_fusion.7 = f32[2432]{0:T(1024)S(1)} fusion(f32[1970]{0:T(1024)S(1)} %reshape.406, s32[3072]{0:T(1024)S(1)} %get-tuple-element.164), kind=kCustom, calls=%fused_computation.4.clone | custom fusion | bytes 29184 | tf_op jit(solution)/shard_map/jit(_take)/gather | solution.py:173
  501.6 55.1 %all-to-all-done.4 = bf16[304,8,512]{2,0,1:T(8,128)(2,1)S(1)} async-done(((bf16[304,8,512]{2,0,1:T(8,128)(2,1)}), bf16[304,8,512]{2,0,1:T(8,128)(2,1)S(1)}, u32[]{:S(2)}, u32[]{:S(2)}) %all-to-all-start.4) | async-done | bytes 2490400 | tf_op jit(solution)/shard_map/all_to_all | solution.py:53
  556.6 10.6 fusion.15
  579.4 25.6 %reduce-scatter.9.cloned.1.call-done = bf16[76,8,512]{2,1,0:T(8,128)(2,1)} async-done(((bf16[304,8,512]{2,1,0:T(8,128)(2,1)}), bf16[76,8,512]{2,1,0:T(8,128)(2,1)}) %reduce-scatter.9.cloned.1.call-update) | async-done | bytes 622608 | tf_op jit(solution)/shard_map/reduce_scatter | solution.py:61
  605.1 26.5 %all-gather.9.cloned.1.call-done = bf16[304,8,512]{2,1,0:T(8,128)(2,1)} async-done(((bf16[76,8,512]{2,1,0:T(8,128)(2,1)}), bf16[304,8,512]{2,1,0:T(8,128)(2,1)}) %all-gather.9.cloned.1.call-update) | async-done | bytes 2490384 | tf_op jit(solution)/shard_map/all_gather | solution.py:69
  637.7 4.8 all-to-all-start.5
  648.1 9.3 gather_fusion.5
  657.3 5.1 reshape.588
  662.5 37.3 %all-to-all-done.5 = bf16[304,8,512]{2,0,1:T(8,128)(2,1)} async-done(((bf16[304,8,512]{2,0,1:T(8,128)(2,1)}), bf16[304,8,512]{2,0,1:T(8,128)(2,1)}, u32[]{:S(2)}, u32[]{:S(2)}) %all-to-all-start.5) | async-done | bytes 2490400 | tf_op jit(solution)/shard_map/all_to_all | solution.py:70
  702.8 9.1 gather_fusion.8
  712.0 5.3 reshape.596
  717.3 22.2 %multiply_reduce_fusion.3 = (f32[985,2]{1,0:T(8,128)}, f32[985,512]{1,0:T(8,128)}, f32[985,512]{1,0:T(8,128)}) fusion(f32[985,512]{1,0:T(8,128)S(1)} %copy-done.1, f32[985,2]{1,0:T(8,128)S(1)} %convert_element_type.237, bf16[985,2,512]{2,1,0:T(2,128)(2,1)} %reshape.588, pred[985,2]{1,0:T(8,128)(4,1)S(1)} %copy-done.75, f32[985,2]{1,0:T(8,128)S(1)} %copy.431, ...), kind=kLoop, calls=%fused_computation.47 | loop fusion | flops 10084430 | bytes 10112010 | tf_op jit(solution)/shard_map/reduce_sum | solution.py:160
  761.5 13.0 %gather_fusion.10 = f32[2432]{0:T(1024)S(1)} fusion(f32[1970]{0:T(1024)S(1)} %reshape.411, s32[3072]{0:T(1024)S(1)} %copy-done.108), kind=kCustom, calls=%fused_computation.11.clone | custom fusion | bytes 29184 | tf_op jit(solution)/shard_map/jit(_take)/gather | solution.py:173
  774.6 20.7 %all-reduce.14.cloned.1.call-done = bf16[985,512]{1,0:T(8,128)(2,1)} async-done(((bf16[985,512]{1,0:T(8,128)(2,1)}), bf16[985,512]{1,0:T(8,128)(2,1)}) %all-reduce.14.cloned.1.call-update) | async-done | bytes 1008656 | tf_op jit(solution)/shard_map/psum | solution.py:234
  800.0 7.5 gather_fusion.9
  812.7 61.8 %all_to_all.46 = bf16[304,8,512]{2,0,1:T(8,128)(2,1)S(1)} all-to-all(bf16[304,8,512]{2,0,1:T(8,128)(2,1)S(1)} %copy.470), channel_id=1, replica_groups=mesh['expert'=8,'tensor'=4] {'expert'}, dimensions={1} | all-to-all | bytes 4980736 | tf_op jit(solution)/shard_map/all_to_all | solution.py:53
  876.0 7.3 fusion.8
  887.9 32.5 %reduce-scatter.11.cloned.1.call-done = bf16[76,8,512]{2,1,0:T(8,128)(2,1)} async-done(((bf16[304,8,512]{2,1,0:T(8,128)(2,1)}), bf16[76,8,512]{2,1,0:T(8,128)(2,1)}) %reduce-scatter.11.cloned.1.call-update) | async-done | bytes 622608 | tf_op jit(solution)/shard_map/reduce_scatter | solution.py:61
  920.4 26.5 %all-gather.11.cloned.1.call-done = bf16[304,8,512]{2,1,0:T(8,128)(2,1)} async-done(((bf16[76,8,512]{2,1,0:T(8,128)(2,1)}), bf16[304,8,512]{2,1,0:T(8,128)(2,1)}) %all-gather.11.cloned.1.call-update) | async-done | bytes 2490384 | tf_op jit(solution)/shard_map/all_gather | solution.py:69
  951.0 5.5 all-to-all-start.7
  961.4 7.0 fusion.105
  981.9 31.8 %all-to-all-done.7 = bf16[304,8,512]{2,0,1:T(8,128)(2,1)} async-done(((bf16[304,8,512]{2,0,1:T(8,128)(2,1)}), bf16[304,8,512]{2,0,1:T(8,128)(2,1)}, u32[]{:S(2)}, u32[]{:S(2)}) %all-to-all-start.7) | async-done | bytes 2490400 | tf_op jit(solution)/shard_map/all_to_all | solution.py:70
  1013.7 4.5 copy.581
  1018.2 11.4 gather_fusion.11
  1029.6 5.2 reshape.604
  1034.8 18.7 %multiply_reduce_fusion.1 = (f32[985,2]{1,0:T(8,128)}, f32[985,512]{1,0:T(8,128)}) fusion(f32[985,512]{1,0:T(8,128)S(1)} %fusion.91, f32[985,2]{1,0:T(8,128)S(1)} %copy-done.33, bf16[985,2,512]{2,1,0:T(2,128)(2,1)} %copy-done.24, pred[985,2]{1,0:T(8,128)(4,1)} %copy.414, bf16[985,2,512]{2,1,0:T(2,128)(2,1)} %reshape.604), kind=kLoop, calls=%fused_computation.45 | loop fusion | flops 8571470 | bytes 8086850 | tf_op jit(solution)/shard_map/reduce_sum | solution.py:160
  1089.4 27.4 %all-reduce.16.cloned.1.call-done = bf16[985,512]{1,0:T(8,128)(2,1)} async-done(((bf16[985,512]{1,0:T(8,128)(2,1)}), bf16[985,512]{1,0:T(8,128)(2,1)}) %all-reduce.16.cloned.1.call-update) | async-done | bytes 1008656 | tf_op jit(solution)/shard_map/psum | solution.py:234
  1119.3 39.9 %all-reduce.2 = (f32[2,2,512]{2,1,0:T(2,128)}, f32[2,2,512]{2,0,1:T(2,128)S(1)}, f32[2,512,8]{1,2,0:T(8,128)}) all-reduce(f32[2,2,512]{2,1,0:T(2,128)S(1)} %pad_maximum_fusion.3, f32[2,2,512]{2,0,1:T(2,128)S(1)} %pad_maximum_fusion.4, f32[2,512,8]{1,2,0:T(8,128)S(1)} %pad_maximum_fusion.2), channel_id=1, replica_groups=mesh['expert'=8,'tensor'=4] {'expert'}, use_global_device_ids=true, to_apply=%region_58.64 | all-reduce | flops 12288 | bytes 98304 | tf_op jit(solution)/shard_map/psum | solution.py:286
  1162.8 61.7 %all-reduce.18.cloned.1.call-done = (f32[2,3,512,128]{2,3,1,0:T(8,128)}, f32[2,128,512]{2,1,0:T(8,128)}) async-done(((f32[2,3,512,128]{2,3,1,0:T(8,128)}, f32[2,128,512]{2,1,0:T(8,128)}), (f32[2,3,512,128]{2,3,1,0:T(8,128)}, f32[2,128,512]{2,1,0:T(8,128)})) %all-reduce.18.cloned.1.call-update) | async-done | bytes 2097168 | tf_op jit(solution)/shard_map/psum | solution.py:286
  (596 shorter events, 239.5 us)
Async XLA Ops:
  7.2 55.8 %all-reduce.10.cloned.1.call-start = ((), (), s32[]{:S(2)}) async-start(), calls=%async_computation.12 | async-start | bytes 2031616 | tf_op jit(solution)/shard_map/psum | solution.py:102
  11.1 54.1 %copy-start.134 = (f32[1,1,512]{2,1,0:T(1,128)}, f32[1,1,512]{2,1,0:T(1,128)S(1)}, u32[]{:S(2)}) copy-start(f32[1,1,512]{2,1,0:T(1,128)S(1)} %get-tuple-element.146) | copy-start | bytes 6148
  24.2 157.6 %reduce-scatter.5.cloned.1.call-start = ((), (), s32[]{:S(2)}) async-start(), calls=%async_computation.13 | async-start | bytes 3112960 | tf_op jit(solution)/shard_map/reduce_scatter | solution.py:61
  38.9 26.4 %copy-start.84 = (s32[2432]{0:T(1024)}, s32[2432]{0:T(1024)S(1)}, u32[]{:S(2)}) copy-start(s32[2432]{0:T(1024)S(1)} %scatter_custom_fusion.1) | copy-start | bytes 29188
  50.1 24.5 %copy-start.128 = (pred[2432]{0:T(1024)(128)(4,1)}, pred[2432]{0:T(1024)(128)(4,1)S(1)}, u32[]{:S(2)}) copy-start(pred[2432]{0:T(1024)(128)(4,1)S(1)} %scatter_custom_fusion) | copy-start | bytes 7300
  50.2 24.4 %copy-start.124 = (pred[2432]{0:T(1024)(128)(4,1)}, pred[2432]{0:T(1024)(128)(4,1)S(1)}, u32[]{:S(2)}) copy-start(pred[2432]{0:T(1024)(128)(4,1)S(1)} %get-tuple-element.123) | copy-start | bytes 7300
  66.4 163.0 %copy-start.2 = (bf16[985,512]{1,0:T(8,128)(2,1)}, bf16[985,512]{1,0:T(8,128)(2,1)S(1)}, u32[]{:S(2)}) copy-start(bf16[985,512]{1,0:T(8,128)(2,1)S(1)} %add_convert_fusion.3) | copy-start | bytes 3025924
  78.9 63.3 %copy-start.67 = (bf16[2,1,512,512]{3,2,1,0:T(8,128)(2,1)S(1)}, bf16[2,1,512,512]{3,2,1,0:T(8,128)(2,1)}, u32[]{:S(2)}) copy-start(bf16[2,1,512,512]{3,2,1,0:T(8,128)(2,1)} %param.27) | copy-start | bytes 3145732
  149.3 59.0 %all-gather.5.cloned.1.call-start = ((), (), s32[]{:S(2)}) async-start(), calls=%async_computation.14 | async-start | bytes 3112960 | tf_op jit(solution)/shard_map/all_gather | solution.py:69
  212.3 62.7 %all-to-all-start.1 = ((bf16[304,8,512]{2,0,1:T(8,128)(2,1)}), bf16[304,8,512]{2,0,1:T(8,128)(2,1)}, u32[]{:S(2)}, u32[]{:S(2)}) async-start(bf16[304,8,512]{2,0,1:T(8,128)(2,1)} %copy.418), calls=%async_computation.2 | async-start | bytes 4980736 | tf_op jit(solution)/shard_map/all_to_all | solution.py:70
  217.8 144.7 %all-reduce.12.cloned.1.call-start = ((), (), s32[]{:S(2)}) async-start(), calls=%async_computation.15 | async-start | bytes 2031616 | tf_op jit(solution)/shard_map/psum | solution.py:102
  229.4 48.6 %copy-start.6 = (s32[2048]{0:T(1024)}, s32[2048]{0:T(1024)S(1)}, u32[]{:S(2)}) copy-start(s32[2048]{0:T(1024)S(1)} %pad_clamp_fusion.5) | copy-start | bytes 24580
  249.9 41.6 %copy-start.34 = (f32[985,2]{1,0:T(8,128)}, f32[985,2]{1,0:T(8,128)S(1)}, u32[]{:S(2)}) copy-start(f32[985,2]{1,0:T(8,128)S(1)} %copy.410) | copy-start | bytes 23644
  314.6 47.9 %copy-start.11 = (f32[985,512]{1,0:T(8,128)}, f32[985,512]{1,0:T(8,128)S(1)}, u32[]{:S(2)}) copy-start(f32[985,512]{1,0:T(8,128)S(1)} %get-tuple-element.120) | copy-start | bytes 6051844
  326.9 37.1 %copy-start.47 = (bf16[985,128]{0,1:T(8,128)(2,1)}, bf16[985,128]{0,1:T(8,128)(2,1)S(1)}, u32[]{:S(2)}) copy-start(bf16[985,128]{0,1:T(8,128)(2,1)S(1)} %convert_element_type.229) | copy-start | bytes 756484
  328.4 172.6 %reduce-scatter.7.cloned.1.call-start = ((), (), s32[]{:S(2)}) async-start(), calls=%async_computation.16 | async-start | bytes 3112960 | tf_op jit(solution)/shard_map/reduce_scatter | solution.py:61
  339.8 34.0 %copy-start.130 = (pred[2432]{0:T(1024)(128)(4,1)}, pred[2432]{0:T(1024)(128)(4,1)S(1)}, u32[]{:S(2)}) copy-start(pred[2432]{0:T(1024)(128)(4,1)S(1)} %scatter_custom_fusion.2) | copy-start | bytes 7300
  349.8 107.2 %copy-start.87 = (s32[2432]{0:T(1024)}, s32[2432]{0:T(1024)S(1)}, u32[]{:S(2)}) copy-start(s32[2432]{0:T(1024)S(1)} %scatter_custom_fusion.3) | copy-start | bytes 29188
  349.9 24.0 %copy-start.126 = (pred[2432]{0:T(1024)(128)(4,1)}, pred[2432]{0:T(1024)(128)(4,1)S(1)}, u32[]{:S(2)}) copy-start(pred[2432]{0:T(1024)(128)(4,1)S(1)} %get-tuple-element.115) | copy-start | bytes 7300
  365.7 91.9 %copy-start.4 = (bf16[985,512]{1,0:T(8,128)(2,1)}, bf16[985,512]{1,0:T(8,128)(2,1)S(1)}, u32[]{:S(2)}) copy-start(bf16[985,512]{1,0:T(8,128)(2,1)S(1)} %add_convert_fusion.1) | copy-start | bytes 3025924
  376.4 63.2 %copy-start.68 = (bf16[2,1,512,512]{3,2,1,0:T(8,128)(2,1)S(1)}, bf16[2,1,512,512]{3,2,1,0:T(8,128)(2,1)}, u32[]{:S(2)}) copy-start(bf16[2,1,512,512]{3,2,1,0:T(8,128)(2,1)} %param.27) | copy-start | bytes 3145732
  497.3 59.3 %all-to-all-start.4 = ((bf16[304,8,512]{2,0,1:T(8,128)(2,1)}), bf16[304,8,512]{2,0,1:T(8,128)(2,1)S(1)}, u32[]{:S(2)}, u32[]{:S(2)}) async-start(bf16[304,8,512]{2,0,1:T(8,128)(2,1)} %copy.446), calls=%async_computation.6 | async-start | bytes 4980736 | tf_op jit(solution)/shard_map/all_to_all | solution.py:53
  500.9 70.9 %all-gather.7.cloned.1.call-start = ((), (), s32[]{:S(2)}) async-start(), calls=%async_computation.17 | async-start | bytes 3112960 | tf_op jit(solution)/shard_map/all_gather | solution.py:69
  501.5 103.5 %reduce-scatter.9.cloned.1.call-start = ((), (), s32[]{:S(2)}) async-start(), calls=%async_computation.18 | async-start | bytes 3112960 | tf_op jit(solution)/shard_map/reduce_scatter | solution.py:61
  575.7 60.5 %all-to-all-start.3 = ((bf16[304,8,512]{2,0,1:T(8,128)(2,1)}), bf16[304,8,512]{2,0,1:T(8,128)(2,1)S(1)}, u32[]{:S(2)}, u32[]{:S(2)}) async-start(bf16[304,8,512]{2,0,1:T(8,128)(2,1)} %copy.439), calls=%async_computation.5 | async-start | bytes 4980736 | tf_op jit(solution)/shard_map/all_to_all | solution.py:70
  579.4 52.1 %all-gather.9.cloned.1.call-start = ((), (), s32[]{:S(2)}) async-start(), calls=%async_computation.19 | async-start | bytes 3112960 | tf_op jit(solution)/shard_map/all_gather | solution.py:69
  637.7 62.0 %all-to-all-start.5 = ((bf16[304,8,512]{2,0,1:T(8,128)(2,1)}), bf16[304,8,512]{2,0,1:T(8,128)(2,1)}, u32[]{:S(2)}, u32[]{:S(2)}) async-start(bf16[304,8,512]{2,0,1:T(8,128)(2,1)} %copy.448), calls=%async_computation.8 | async-start | bytes 4980736 | tf_op jit(solution)/shard_map/all_to_all | solution.py:70
  642.6 152.7 %all-reduce.14.cloned.1.call-start = ((), (), s32[]{:S(2)}) async-start(), calls=%async_computation.20 | async-start | bytes 2031616 | tf_op jit(solution)/shard_map/psum | solution.py:234
  717.3 23.6 %copy-start.92 = (f32[985]{0:T(1024)S(1)}, f32[985]{0:T(1024)}, u32[]{:S(2)}) copy-start(f32[985]{0:T(1024)} %copy-done.91) | copy-start | bytes 11824
  717.3 23.6 %copy-start.101 = (f32[985]{0:T(1024)S(1)}, f32[985]{0:T(1024)}, u32[]{:S(2)}) copy-start(f32[985]{0:T(1024)} %copy-done.100) | copy-start | bytes 11824
  717.3 23.6 %copy-start.111 = (bf16[2,512,8]{1,2,0:T(8,128)(2,1)S(1)}, bf16[2,512,8]{1,2,0:T(8,128)(2,1)}, u32[]{:S(2)}) copy-start(bf16[2,512,8]{1,2,0:T(8,128)(2,1)} %param.26) | copy-start | bytes 49156
  717.3 23.6 %copy-start.121 = (f32[1,1,512]{2,1,0:T(1,128)S(1)}, f32[1,1,512]{2,1,0:T(1,128)}, u32[]{:S(2)}) copy-start(f32[1,1,512]{2,1,0:T(1,128)} %get-tuple-element.145) | copy-start | bytes 6148
  761.1 159.3 %reduce-scatter.11.cloned.1.call-start = ((), (), s32[]{:S(2)}) async-start(), calls=%async_computation.21 | async-start | bytes 3112960 | tf_op jit(solution)/shard_map/reduce_scatter | solution.py:61
  761.5 33.8 %copy-start.12 = (f32[985,512]{1,0:T(8,128)S(1)}, f32[985,512]{1,0:T(8,128)}, u32[]{:S(2)}) copy-start(f32[985,512]{1,0:T(8,128)} %copy-done.11) | copy-start | bytes 6051844
  761.5 33.8 %copy-start.95 = (f32[985]{0:T(1024)S(1)}, f32[985]{0:T(1024)}, u32[]{:S(2)}) copy-start(f32[985]{0:T(1024)} %copy-done.94) | copy-start | bytes 11824
  761.5 33.8 %copy-start.107 = (f32[985]{0:T(1024)S(1)}, f32[985]{0:T(1024)}, u32[]{:S(2)}) copy-start(f32[985]{0:T(1024)} %copy-done.106) | copy-start | bytes 11824
  761.5 33.8 %copy-start.123 = (f32[1,1,512]{2,1,0:T(1,128)S(1)}, f32[1,1,512]{2,1,0:T(1,128)}, u32[]{:S(2)}) copy-start(f32[1,1,512]{2,1,0:T(1,128)} %get-tuple-element.148) | copy-start | bytes 6148
  807.5 68.5 %slice-start = ((s8[4980736]{0:T(1024)(128)(4,1)}), s8[4194304]{0:T(1024)(128)(4,1)S(1)}, s32[]{:S(2)}) async-start(s8[4980736]{0:T(1024)(128)(4,1)} %bitcast.326), calls=%async_computation.25 | async-start | bytes 8388608
  811.8 64.2 %slice-start.1 = ((s8[4980736]{0:T(1024)(128)(4,1)}), s8[786432]{0:T(1024)(128)(4,1)S(1)}, s32[]{:S(2)}) async-start(s8[4980736]{0:T(1024)(128)(4,1)} %bitcast.326), calls=%async_computation.26 | async-start | bytes 1572864
  812.7 63.3 %copy-start.155 = (bf16[2,1,512,512]{3,2,1,0:T(8,128)(2,1)S(1)}, bf16[2,1,512,512]{3,2,1,0:T(8,128)(2,1)}, u32[]{:S(2)}) copy-start(bf16[2,1,512,512]{3,2,1,0:T(8,128)(2,1)} %param.28) | copy-start | bytes 3145732
  887.8 59.1 %all-gather.11.cloned.1.call-start = ((), (), s32[]{:S(2)}) async-start(), calls=%async_computation.22 | async-start | bytes 3112960 | tf_op jit(solution)/shard_map/all_gather | solution.py:69
  951.0 62.7 %all-to-all-start.7 = ((bf16[304,8,512]{2,0,1:T(8,128)(2,1)}), bf16[304,8,512]{2,0,1:T(8,128)(2,1)}, u32[]{:S(2)}, u32[]{:S(2)}) async-start(bf16[304,8,512]{2,0,1:T(8,128)(2,1)} %copy.472), calls=%async_computation.11 | async-start | bytes 4980736 | tf_op jit(solution)/shard_map/all_to_all | solution.py:70
  956.5 160.3 %all-reduce.16.cloned.1.call-start = ((), (), s32[]{:S(2)}) async-start(), calls=%async_computation.23 | async-start | bytes 2031616 | tf_op jit(solution)/shard_map/psum | solution.py:234
  981.9 36.3 %copy-start.7 = (s32[2048]{0:T(1024)S(1)}, s32[2048]{0:T(1024)}, u32[]{:S(2)}) copy-start(s32[2048]{0:T(1024)} %copy-done.6) | copy-start | bytes 24580
  1082.6 141.8 %all-reduce.18.cloned.1.call-start = ((), (), s32[]{:S(2)}) async-start(), calls=%async_computation.24 | async-start | bytes 4194304 | tf_op jit(solution)/shard_map/psum | solution.py:286
  1089.1 30.2 %copy-start.140 = (f32[1,2,512]{2,1,0:T(2,128)S(1)}, f32[1,2,512]{2,1,0:T(2,128)}, u32[]{:S(2)}) copy-start(f32[1,2,512]{2,1,0:T(2,128)} %maximum_bitcast_fusion.3) | copy-start | bytes 12292
  1089.1 30.2 %copy-start.139 = (f32[1,2,512]{2,0,1:T(1,128)S(1)}, f32[1,2,512]{2,0,1:T(1,128)}, u32[]{:S(2)}) copy-start(f32[1,2,512]{2,0,1:T(1,128)} %stack.147) | copy-start | bytes 12292
  1089.1 70.7 %copy-start.18 = (f32[985,512]{1,0:T(8,128)S(1)}, f32[985,512]{1,0:T(8,128)}, u32[]{:S(2)}) copy-start(f32[985,512]{1,0:T(8,128)} %copy-done.17) | copy-start | bytes 6051844
  (133 other events, 593.9 us)
Sparse Core Ops, SparseCore 0:
  24.4 38.5 all-reduce.9
  149.4 32.3 reduce-scatter.4
  183.4 24.8 all-gather.4
  328.5 34.0 all-reduce.11
  447.0 32.3 reduce-scatter.6
  503.0 26.0 all-gather.6
  571.9 33.1 reduce-scatter.8
  606.7 24.8 all-gather.8
  761.3 34.0 all-reduce.13
  888.0 32.4 reduce-scatter.10
  922.0 24.7 all-gather.10
  1082.8 33.9 all-reduce.15
  1121.0 103.4 all-reduce.17
where the time goes:
time: 1240 us
  waiting for transfers between devices  456 us (37%)
  local copies, waits for them, and re-layouts  307 us (25%)
  blocking collectives  225 us (18%)
  other arithmetic  119 us (10%)
  matrix products  86.4 us (7%)
  starting transfers between devices  24.3 us (2%)
  between operations  16.9 us (1%)
    all_to_all x3, blocking collectives, to_experts(): lax.all_to_all(slot_rows, 'expert', split_axis=1, concat_axis=1, tiled=True)  185 us
    all_to_all x4, waiting for transfers between devices, return_rows(): lax.all_to_all(whole_rows, 'expert', split_axis=1, concat_axis=1, tiled=T...  94.8 us
    reduce_scatter x4, waiting for transfers between devices, return_rows(): lax.psum_scatter(product.reshape(per_rank * lax.axis_size('tensor'), expe...  90.7 us
    all_gather x4, waiting for transfers between devices, return_rows(): whole_rows = lax.all_gather(share_rows, 'tensor', axis=0, tiled=True)  79.3 us
    psum x1, waiting for transfers between devices, body(): lax.psum((stacked[0], stacked[1], stacked[2], stacked[3], stacked[4]), 'e...  61.7 us
    all_to_all x1, waiting for transfers between devices, to_experts(): lax.all_to_all(slot_rows, 'expert', split_axis=1, concat_axis=1, tiled=True)  55.1 us
    psum x2, waiting for transfers between devices, layer_backward(): lax.psum(input_part.astype(jnp.bfloat16), 'tensor').astype(jnp.float32)  48.1 us
    reduce_sum x2, other arithmetic, layer_backward(): gate_grad = jnp.sum(grad_stream[:, None, :] * saved['picked'], -1)  40.9 us
  transfers between devices with their start and end apart: 18, of which 16 were waited for; matrix products, arithmetic and copies ran while one was open for 18% of the time, Pallas kernels for 0%

commit v1 on v0

v1 whole, which is shorter than its diff:
```python
import functools

import jax
import jax.numpy as jnp
from jax import lax
from jax.experimental import pallas as pl
from jax.experimental.pallas import tpu as pltpu
from jax.sharding import PartitionSpec as P

HEAD_DIM = 64
SEQ = 197
PAD = 208
LAYERS = 2
EPS = 1e-06
MESH = pl.DeviceIdType.MESH
F32 = jnp.float32
BF16 = jnp.bfloat16
SCALE = HEAD_DIM ** (-0.5)
MIB = 1 << 20


def up_to(count, multiple):
    return -(-count // multiple) * multiple


def dot(left, right):
    return lax.dot_general(left, right, (((1,), (0,)), ((), ())), preferred_element_type=F32)


def dot_nt(left, right):
    return lax.dot_general(left, right, (((1,), (1,)), ((), ())), preferred_element_type=F32)


def dot_tn(left, right):
    return lax.dot_general(left, right, (((0,), (0,)), ((), ())), preferred_element_type=F32)


def norm_parts(rows):
    centered = rows - jnp.mean(rows, -1, keepdims=True)
    scaled = lax.rsqrt(jnp.mean(centered * centered, -1, keepdims=True) + EPS)
    return centered * scaled, scaled


def norm_pull(grad_in, normed, scaled, gain_row):
    grad_normed = grad_in * gain_row
    inner = (
        grad_normed
        - jnp.mean(grad_normed, -1, keepdims=True)
        - normed * jnp.mean(grad_normed * normed, -1, keepdims=True)
    )
    return inner * scaled


def tensor_place():
    place = lax.axis_index("tensor")
    core = lax.rem(place, 2)
    core_peer = place + 1 - 2 * core
    chip_peer = lax.rem(place + 2, 4)
    return place, core, core_peer, chip_peer


def greet_tensor(core_peer, chip_peer):
    barrier = pltpu.get_barrier_semaphore()
    for peer in (core_peer, chip_peer):
        pl.semaphore_signal(barrier, inc=1, device_id={"tensor": peer}, device_id_type=MESH)


def greet_expert(size):
    me = lax.axis_index("expert")
    barrier = pltpu.get_barrier_semaphore()

    def one(step, carry):
        peer = lax.rem(me + step, size)
        pl.semaphore_signal(barrier, inc=1, device_id={"expert": peer}, device_id_type=MESH)
        return carry

    lax.fori_loop(1, size, one, 0)


class TensorSum:
    def __init__(self, part, near, chip_sum, far, final, send, recv):
        self.part, self.near, self.chip_sum, self.far, self.final = part, near, chip_sum, far, final
        self.send, self.recv = send, recv
        _, self.core, self.core_peer, self.chip_peer = tensor_place()

    @staticmethod
    def scratch(images):
        rows = images * PAD
        half = (rows, 256)
        return [
            pltpu.VMEM((2,) + half, BF16),
            pltpu.VMEM(half, BF16),
            pltpu.VMEM(half, BF16),
            pltpu.VMEM(half, BF16),
            pltpu.VMEM((2,) + half, BF16),
            pltpu.SemaphoreType.DMA((3, images)),
            pltpu.SemaphoreType.DMA((3, images)),
        ]

    def rows(self, image):
        return pl.ds(pl.multiple_of(image * PAD, PAD), PAD)

    def first(self, image):
        rows = self.rows(image)
        return pltpu.make_async_remote_copy(
            src_ref=self.part.at[1 - self.core, rows],
            dst_ref=self.near.at[rows],
            send_sem=self.send.at[0, image],
            recv_sem=self.recv.at[0, image],
            device_id={"tensor": self.core_peer},
            device_id_type=MESH,
        )

    def second(self, image):
        rows = self.rows(image)
        return pltpu.make_async_remote_copy(
            src_ref=self.chip_sum.at[rows],
            dst_ref=self.far.at[rows],
            send_sem=self.send.at[1, image],
            recv_sem=self.recv.at[1, image],
            device_id={"tensor": self.chip_peer},
            device_id_type=MESH,
        )

    def third(self, image):
        rows = self.rows(image)
        return pltpu.make_async_remote_copy(
            src_ref=self.final.at[self.core, rows],
            dst_ref=self.final.at[self.core, rows],
            send_sem=self.send.at[2, image],
            recv_sem=self.recv.at[2, image],
            device_id={"tensor": self.core_peer},
            device_id_type=MESH,
        )

    def put(self, image, value):
        rows = self.rows(image)
        self.part[0, rows, :] = value[:, :256].astype(BF16)
        self.part[1, rows, :] = value[:, 256:].astype(BF16)

    def step_near(self, image):
        rows = self.rows(image)
        self.first(image).wait()
        self.chip_sum[rows, :] = (
            self.part[self.core, rows, :].astype(F32) + self.near[rows, :].astype(F32)
        ).astype(BF16)
        self.second(image).start()

    def step_far(self, image):
        rows = self.rows(image)
        self.second(image).wait()
        self.final[self.core, rows, :] = (
            self.chip_sum[rows, :].astype(F32) + self.far[rows, :].astype(F32)
        ).astype(BF16)
        self.third(image).start()

    def step_end(self, image):
        self.third(image).wait()

    def get(self, image):
        rows = self.rows(image)
        return jnp.concatenate(
            [self.final[0, rows, :].astype(F32), self.final[1, rows, :].astype(F32)], axis=1
        )


def finish_sum(total, images, use):
    def far(image, carry):
        total.step_far(image)
        return carry

    def body(image, carry):
        total.step_far(image)
        total.step_end(image - 1)
        use(image - 1, total.get(image - 1))
        return carry

    total.step_far(0)
    lax.fori_loop(1, images, body, 0)
    total.step_end(images - 1)
    use(images - 1, total.get(images - 1))


class Exchange:
    def __init__(self, size, block, src, dst, send, recv, local):
        self.size, self.block, self.src, self.dst = size, block, src, dst
        self.send, self.recv, self.local = send, recv, local
        self.me = lax.axis_index("expert")

    @staticmethod
    def scratch(size):
        return [
            pltpu.SemaphoreType.DMA((size,)),
            pltpu.SemaphoreType.DMA((size,)),
            pltpu.SemaphoreType.DMA,
        ]

    def rows(self, index):
        return pl.ds(pl.multiple_of(index * self.block, self.block), self.block)

    def own(self):
        return pltpu.make_async_copy(
            self.src.at[self.rows(self.me)], self.dst.at[self.rows(self.me)], self.local
        )

    def copy(self, step):
        target = lax.rem(self.me + step, self.size)
        return pltpu.make_async_remote_copy(
            src_ref=self.src.at[self.rows(target)],
            dst_ref=self.dst.at[self.rows(self.me)],
            send_sem=self.send.at[step],
            recv_sem=self.recv.at[step],
            device_id={"expert": target},
            device_id_type=MESH,
        )

    def start(self):
        def one(step, carry):
            self.copy(step).start()
            return carry

        lax.fori_loop(1, self.size, one, 0)
        self.own().start()

    def wait(self):
        def one(step, carry):
            self.copy(step).wait()
            return carry

        self.own().wait()
        lax.fori_loop(1, self.size, one, 0)


def attend_forward(images, refs):
    (
        x_ref, gain_ref, bias_ref, wqkv_ref, wout_ref,
        y_ref, h_ref, qkv_ref, prob_ref, mixed_ref,
    ) = refs[:10]
    total = TensorSum(*refs[10:])
    greet_tensor(total.core_peer, total.chip_peer)
    joint = jnp.concatenate([wqkv_ref[0], wqkv_ref[1], wqkv_ref[2]], axis=1)
    w_out = wout_ref[...]
    first_head = lax.broadcasted_iota(jnp.int32, (PAD, 2 * HEAD_DIM), 1) < HEAD_DIM
    key_real = lax.broadcasted_iota(jnp.int32, (2 * PAD, PAD), 1) < SEQ
    nothing = jnp.zeros((PAD, 2 * HEAD_DIM), BF16)

    def compute(image):
        rows = total.rows(image)
        normed, _ = norm_parts(x_ref[rows, :])
        hidden = (normed * gain_ref[0:1, :] + bias_ref[0:1, :]).astype(BF16)
        h_ref[rows, :] = hidden
        proj = dot(hidden, joint).astype(BF16)
        qkv_ref[rows, :] = proj
        query, keyed, valued = proj[:, :128], proj[:, 128:256], proj[:, 256:]
        both = jnp.concatenate(
            [jnp.where(first_head, query, nothing), jnp.where(first_head, nothing, query)], axis=0
        )
        scores = jnp.where(key_real, dot_nt(both, keyed) * SCALE, -1e30)
        expd = jnp.exp(scores - jnp.max(scores, -1, keepdims=True))
        prob = (expd / jnp.sum(expd, -1, keepdims=True)).astype(BF16)
        prob_ref[image] = prob
        out = dot(prob, valued)
        mixed = jnp.where(first_head, out[:PAD], out[PAD:]).astype(BF16)
        mixed_ref[rows, :] = mixed
        total.put(image, dot(mixed, w_out))

    def body(image, carry):
        compute(image)
        total.first(image).start()
        total.step_near(image - 1)
        return carry

    compute(0)
    pl.semaphore_wait(pltpu.get_barrier_semaphore(), 2)
    total.first(0).start()
    lax.fori_loop(1, images, body, 0)
    total.step_near(images - 1)

    def use(image, value):
        rows = total.rows(image)
        y_ref[rows, :] = x_ref[rows, :] + value

    finish_sum(total, images, use)


def attention_forward(x, gain, bias, w_qkv, w_out, collective_id):
    rows = x.shape[0]
    images = rows // PAD

    def kernel(*refs):
        attend_forward(images, refs)

    return pl.pallas_call(
        kernel,
        name="attention_forward",
        out_shape=(
            jax.ShapeDtypeStruct((rows, 512), F32),
            jax.ShapeDtypeStruct((rows, 512), BF16),
            jax.ShapeDtypeStruct((rows, 384), BF16),
            jax.ShapeDtypeStruct((images, 2 * PAD, PAD), BF16),
            jax.ShapeDtypeStruct((rows, 128), BF16),
        ),
        scratch_shapes=TensorSum.scratch(images),
        compiler_params=pltpu.CompilerParams(
            collective_id=collective_id, has_side_effects=True, vmem_limit_bytes=40 * MIB
        ),
    )(x, gain, bias, w_qkv, w_out)


def attend_backward(images, refs):
    (
        g_ref, x_ref, h_ref, qkv_ref, prob_ref, mixed_ref, gain_ref, wqkv_ref, wout_ref,
        gin_ref, gqkv_ref, gout_ref, gvec_ref, low_ref, dproj_ref,
    ) = refs[:15]
    total = TensorSum(*refs[15:])
    greet_tensor(total.core_peer, total.chip_peer)
    joint = jnp.concatenate([wqkv_ref[0], wqkv_ref[1], wqkv_ref[2]], axis=1)
    w_out = wout_ref[...]
    first_head = lax.broadcasted_iota(jnp.int32, (PAD, 2 * HEAD_DIM), 1) < HEAD_DIM
    nothing = jnp.zeros((PAD, 2 * HEAD_DIM), BF16)

    def split(value):
        return jnp.concatenate(
            [jnp.where(first_head, value, nothing), jnp.where(first_head, nothing, value)], axis=0
        )

    def compute(image):
        rows = total.rows(image)
        out_low = g_ref[rows, :].astype(BF16)
        low_ref[rows, :] = out_low
        proj = qkv_ref[rows, :]
        query, keyed, valued = proj[:, :128], proj[:, 128:256], proj[:, 256:]
        mixed_grad = split(dot_nt(out_low, w_out).astype(BF16))
        prob_low = prob_ref[image]
        prob = prob_low.astype(F32)
        prob_grad = dot_nt(mixed_grad, valued)
        score_grad = (
            prob * (prob_grad - jnp.sum(prob_grad * prob, -1, keepdims=True))
        ).astype(BF16)
        query_both = dot(score_grad, keyed)
        query_grad = jnp.where(first_head, query_both[:PAD], query_both[PAD:]) * SCALE
        key_grad = dot_tn(score_grad, split(query)) * SCALE
        value_grad = dot_tn(prob_low, mixed_grad)
        proj_grad = jnp.concatenate([query_grad, key_grad, value_grad], axis=1).astype(BF16)
        dproj_ref[rows, :] = proj_grad
        total.put(image, dot_nt(proj_grad, joint))

    def body(image, carry):
        compute(image)
        total.first(image).start()
        total.step_near(image - 1)
        return carry

    compute(0)
    pl.semaphore_wait(pltpu.get_barrier_semaphore(), 2)
    total.first(0).start()
    lax.fori_loop(1, images, body, 0)
    total.step_near(images - 1)
    gout_ref[...] = dot_tn(mixed_ref[...], low_ref[...])
    gqkv_ref[...] = dot_tn(h_ref[...], dproj_ref[...])
    gvec_ref[...] = jnp.zeros_like(gvec_ref)

    def use(image, value):
        rows = total.rows(image)
        normed, scaled = norm_parts(x_ref[rows, :])
        gin_ref[rows, :] = g_ref[rows, :] + norm_pull(value, normed, scaled, gain_ref[0:1, :])
        gvec_ref[0:1, :] += jnp.sum(value * normed, 0, keepdims=True)
        gvec_ref[1:2, :] += jnp.sum(value, 0, keepdims=True)

    finish_sum(total, images, use)


def attention_backward(grad, x, saved, gain, w_qkv, w_out, collective_id):
    rows = x.shape[0]
    images = rows // PAD
    hidden, qkv, prob, mixed = saved

    def kernel(*refs):
        attend_backward(images, refs)

    return pl.pallas_call(
        kernel,
        name="attention_backward",
        out_shape=(
            jax.ShapeDtypeStruct((rows, 512), F32),
            jax.ShapeDtypeStruct((512, 384), F32),
            jax.ShapeDtypeStruct((128, 512), F32),
            jax.ShapeDtypeStruct((8, 512), F32),
        ),
        scratch_shapes=[pltpu.VMEM((rows, 512), BF16), pltpu.VMEM((rows, 384), BF16)]
        + TensorSum.scratch(images),
        compiler_params=pltpu.CompilerParams(
            collective_id=collective_id, has_side_effects=True, vmem_limit_bytes=48 * MIB
        ),
    )(grad, x, hidden, qkv, prob, mixed, gain, w_qkv, w_out)


class Plan:
    def __init__(self, tok_rows, experts):
        self.images = tok_rows // SEQ
        self.rows = self.images * PAD
        self.lanes = up_to(self.rows, 128)
        self.experts = experts
        self.per_rank = max(1, 10 * tok_rows // (4 * experts * 4))
        self.capacity = 4 * self.per_rank
        self.block = up_to(self.per_rank, 16)
        self.slots = experts * self.block
        self.extra = up_to(experts, 16)


def gelu(pre):
    inner = 0.7978845608028654 * (pre + 0.044715 * (pre * pre * pre))
    return 0.5 * pre * (1.0 + jnp.tanh(inner))


def gelu_both(pre):
    square = pre * pre
    inner = pre * (0.7978845608028654 + 0.035677408136300125 * square)
    bent = jnp.tanh(inner)
    half = 0.5 * (1.0 + bent)
    slope = half + 0.5 * pre * (1.0 - bent * bent) * (
        0.7978845608028654 + 0.10703222440890037 * square
    )
    return half * pre, slope


def build_members(plan, place_ref, gate_ref, member_ref, slot_gate_ref):
    slot = lax.broadcasted_iota(jnp.int32, (plan.block, plan.lanes), 0).astype(F32)

    def one(expert, carry):
        rows = pl.ds(pl.multiple_of(expert * plan.block, plan.block), plan.block)
        hit = place_ref[pl.ds(expert, 1), :] == slot
        member_ref[rows, :] = jnp.where(hit, 1.0, 0.0).astype(BF16)
        slot_gate_ref[rows, :] = jnp.sum(
            jnp.where(hit, gate_ref[pl.ds(expert, 1), :], 0.0), -1, keepdims=True
        )
        return carry

    lax.fori_loop(0, plan.experts, one, 0)


def run_moe_forward(plan, refs):
    (
        y_ref, route_ref, gain_ref, bias_ref, router_ref, up_ref, down_ref,
        next_ref, h2_ref, recv_ref, back_ref, place_ref, gate_ref,
        member_ref, slot_gate_ref, send_ref, ret_ref,
    ) = refs[:17]
    out_move = Exchange(plan.experts, plan.block, send_ref, recv_ref, *refs[17:20])
    back_move = Exchange(plan.experts, plan.block, ret_ref, back_ref, *refs[20:23])
    total = TensorSum(*refs[23:])
    greet_tensor(total.core_peer, total.chip_peer)
    greet_expert(plan.experts)
    rank = lax.axis_index("tensor")

    def norm_body(image, carry):
        rows = total.rows(image)
        normed, _ = norm_parts(y_ref[rows, :])
        h2_ref[rows, :] = (normed * gain_ref[1:2, :] + bias_ref[1:2, :]).astype(BF16)
        return carry

    lax.fori_loop(0, plan.images, norm_body, 0)
    if plan.lanes > plan.rows:
        h2_ref[plan.rows :, :] = jnp.zeros((plan.lanes - plan.rows, 512), BF16)
    hidden = h2_ref[...]
    logits = dot_nt(router_ref[...], hidden)
    shape = (plan.experts, plan.lanes)
    expert_id = lax.broadcasted_iota(jnp.int32, shape, 0)
    named = (expert_id == route_ref[0:1, :]) | (expert_id == route_ref[1:2, :])
    shifted = jnp.where(named, logits, -1e30)
    top = jnp.max(shifted, 0, keepdims=True)
    expd = jnp.where(named, jnp.exp(shifted - top), 0.0)
    share = expd / jnp.maximum(jnp.sum(expd, 0, keepdims=True), 1e-30)
    gate_ref[...] = share
    count = jnp.where(named, 1.0, 0.0)
    lane = lax.broadcasted_iota(jnp.int32, shape, 1)
    running = count
    step = 1
    while step < plan.lanes:
        running = running + jnp.where(lane >= step, pltpu.roll(running, step, 1), 0.0)
        step *= 2
    before = running - count
    mine = before - (rank * plan.per_rank).astype(F32)
    valid = named & (mine >= 0.0) & (mine < float(plan.per_rank))
    place_ref[...] = jnp.where(valid, mine, -1.0)
    build_members(plan, place_ref, gate_ref, member_ref, slot_gate_ref)
    send_ref[...] = dot(member_ref[...], hidden).astype(BF16)
    pl.semaphore_wait(pltpu.get_barrier_semaphore(), 2 + plan.experts - 1)
    out_move.start()
    out_move.wait()
    recv = recv_ref[...]
    result = jnp.zeros((plan.slots, 512), F32)
    for part in range(4):
        hidden_part = gelu(dot(recv, up_ref[part])).astype(BF16)
        result = result + dot(hidden_part, down_ref[part])
    ret_ref[...] = result.astype(BF16)
    back_move.start()
    back_move.wait()
    gated = (back_ref[...].astype(F32) * slot_gate_ref[...]).astype(BF16)
    mixed = dot_tn(member_ref[...], gated)
    for image in range(plan.images):
        total.put(image, mixed[image * PAD : (image + 1) * PAD])

    def go(image, carry):
        total.first(image).start()
        return carry

    def near(image, carry):
        total.step_near(image)
        return carry

    lax.fori_loop(0, plan.images, go, 0)
    lax.fori_loop(0, plan.images, near, 0)

    def use(image, value):
        rows = total.rows(image)
        next_ref[rows, :] = y_ref[rows, :] + value

    finish_sum(total, plan.images, use)


def moe_forward(plan, y, route, gain, bias, router, w_up, w_down, collective_id):
    def kernel(*refs):
        run_moe_forward(plan, refs)

    return pl.pallas_call(
        kernel,
        name="moe_forward",
        out_shape=(
            jax.ShapeDtypeStruct((plan.rows, 512), F32),
            jax.ShapeDtypeStruct((plan.lanes, 512), BF16),
            jax.ShapeDtypeStruct((plan.slots, 512), BF16),
            jax.ShapeDtypeStruct((plan.slots, 512), BF16),
            jax.ShapeDtypeStruct((plan.experts, plan.lanes), F32),
            jax.ShapeDtypeStruct((plan.experts, plan.lanes), F32),
        ),
        scratch_shapes=[
            pltpu.VMEM((plan.slots, plan.lanes), BF16),
            pltpu.VMEM((plan.slots, 1), F32),
            pltpu.VMEM((plan.slots, 512), BF16),
            pltpu.VMEM((plan.slots, 512), BF16),
        ]
        + Exchange.scratch(plan.experts)
        + Exchange.scratch(plan.experts)
        + TensorSum.scratch(plan.images),
        compiler_params=pltpu.CompilerParams(
            collective_id=collective_id, has_side_effects=True, vmem_limit_bytes=56 * MIB
        ),
    )(y, route, gain, bias, router, w_up, w_down)


def run_moe_backward(plan, refs):
    (
        g_ref, y_ref, h2_ref, recv_ref, back_ref, place_ref, gate_ref, gain_ref, router_ref,
        up_ref, down_ref,
        gy_ref, gup_ref, gdown_ref, grouter_ref, gvec_ref,
        member_ref, slot_gate_ref, low_ref, send_ref, drecv_ref, ret_ref, dback_ref,
        act_ref, slope_ref, dpre_ref,
    ) = refs[:26]
    out_move = Exchange(plan.experts, plan.block, send_ref, drecv_ref, *refs[26:29])
    back_move = Exchange(
        plan.experts, plan.block, ret_ref, dback_ref.at[pl.ds(0, plan.slots)], *refs[29:32]
    )
    total = TensorSum(*refs[32:])
    greet_tensor(total.core_peer, total.chip_peer)
    greet_expert(plan.experts)
    low_ref[: plan.rows, :] = g_ref[...].astype(BF16)
    if plan.lanes > plan.rows:
        low_ref[plan.rows :, :] = jnp.zeros((plan.lanes - plan.rows, 512), BF16)
    build_members(plan, place_ref, gate_ref, member_ref, slot_gate_ref)
    members = member_ref.at[pl.ds(0, plan.slots)]
    slot_grad = dot(members[...], low_ref[...])
    send_ref[...] = (slot_grad * slot_gate_ref[...]).astype(BF16)
    pl.semaphore_wait(pltpu.get_barrier_semaphore(), 2 + plan.experts - 1)
    out_move.start()

    product = (slot_grad * back_ref[...].astype(F32)).astype(BF16)
    gate_row = dot_nt(jnp.ones((plan.experts, 512), BF16), product)
    shape = (plan.experts, plan.slots)
    own = lax.broadcasted_iota(jnp.int32, shape, 0) == (
        lax.broadcasted_iota(jnp.int32, shape, 1) // plan.block
    )
    spread = jnp.where(own, gate_row, 0.0)
    spread_high = spread.astype(BF16)
    spread_low = (spread - spread_high.astype(F32)).astype(BF16)
    gate_grad = dot(spread_high, members[...]) + dot(spread_low, members[...])
    share = gate_ref[...]
    logit_grad = share * (gate_grad - jnp.sum(share * gate_grad, 0, keepdims=True))
    logit_low = logit_grad.astype(BF16)
    grouter_ref[...] = dot(logit_low, h2_ref[...])
    member_ref[plan.slots :, :] = jnp.zeros((plan.extra, plan.lanes), BF16)
    member_ref[plan.slots : plan.slots + plan.experts, :] = logit_low
    dback_ref[plan.slots :, :] = jnp.zeros((plan.extra, 512), BF16)
    dback_ref[plan.slots : plan.slots + plan.experts, :] = router_ref[...]
    recv = recv_ref[...]
    for part in range(4):
        act, slope = gelu_both(dot(recv, up_ref[part]))
        act_ref[part] = act.astype(BF16)
        slope_ref[part] = slope.astype(BF16)
    out_move.wait()

    drecv = drecv_ref[...]
    result = jnp.zeros((plan.slots, 512), F32)
    for part in range(4):
        pre_grad = (dot_nt(drecv, down_ref[part]) * slope_ref[part].astype(F32)).astype(BF16)
        dpre_ref[part] = pre_grad
        result = result + dot_nt(pre_grad, up_ref[part])
    ret_ref[...] = result.astype(BF16)
    back_move.start()
    for part in range(4):
        gdown_ref[part] = dot_tn(act_ref[part], drecv).astype(BF16)
        gup_ref[part] = dot_tn(recv, dpre_ref[part]).astype(BF16)
    back_move.wait()

    mixed = dot_tn(member_ref[...], dback_ref[...])
    for image in range(plan.images):
        total.put(image, mixed[image * PAD : (image + 1) * PAD])

    def go(image, carry):
        total.first(image).start()
        return carry

    def near(image, carry):
        total.step_near(image)
        return carry

    lax.fori_loop(0, plan.images, go, 0)
    lax.fori_loop(0, plan.images, near, 0)
    gvec_ref[...] = jnp.zeros_like(gvec_ref)

    def use(image, value):
        rows = total.rows(image)
        normed, scaled = norm_parts(y_ref[rows, :])
        gy_ref[rows, :] = g_ref[rows, :] + norm_pull(value, normed, scaled, gain_ref[1:2, :])
        gvec_ref[0:1, :] += jnp.sum(value * normed, 0, keepdims=True)
        gvec_ref[1:2, :] += jnp.sum(value, 0, keepdims=True)

    finish_sum(total, plan.images, use)


def moe_backward(plan, grad, y, saved, gain, router, w_up, w_down, collective_id):
    h2, recv, back, place, gate = saved

    def kernel(*refs):
        run_moe_backward(plan, refs)

    return pl.pallas_call(
        kernel,
        name="moe_backward",
        out_shape=(
            jax.ShapeDtypeStruct((plan.rows, 512), F32),
            jax.ShapeDtypeStruct((4, 512, 512), BF16),
            jax.ShapeDtypeStruct((4, 512, 512), BF16),
            jax.ShapeDtypeStruct((plan.experts, 512), F32),
            jax.ShapeDtypeStruct((8, 512), F32),
        ),
        scratch_shapes=[
            pltpu.VMEM((plan.slots + plan.extra, plan.lanes), BF16),
            pltpu.VMEM((plan.slots, 1), F32),
            pltpu.VMEM((plan.lanes, 512), BF16),
            pltpu.VMEM((plan.slots, 512), BF16),
            pltpu.VMEM((plan.slots, 512), BF16),
            pltpu.VMEM((plan.slots, 512), BF16),
            pltpu.VMEM((plan.slots + plan.extra, 512), BF16),
            pltpu.VMEM((4, plan.slots, 512), BF16),
            pltpu.VMEM((4, plan.slots, 512), BF16),
            pltpu.VMEM((4, plan.slots, 512), BF16),
        ]
        + Exchange.scratch(plan.experts)
        + Exchange.scratch(plan.experts)
        + TensorSum.scratch(plan.images),
        compiler_params=pltpu.CompilerParams(
            collective_id=collective_id, has_side_effects=True, vmem_limit_bytes=60 * MIB
        ),
    )(grad, y, h2, recv, back, place, gate, gain, router, w_up, w_down)


def body(tokens, routes, ln_gain, ln_bias, w_qkv, w_out, w_router, w_up, w_down, cotangent):
    tok_rows = tokens.shape[0]
    experts = w_router.shape[2]
    plan = Plan(tok_rows, experts)

    def pad_rows(value):
        value = value.astype(F32).reshape(plan.images, SEQ, -1)
        return jnp.pad(value, ((0, 0), (0, PAD - SEQ), (0, 0))).reshape(plan.rows, -1)

    def cut_rows(value):
        return value.reshape(plan.images, PAD, -1)[:, :SEQ].reshape(tok_rows, -1)

    up_all = [lax.all_gather(w_up[layer, 0], "tensor") for layer in range(LAYERS)]
    down_all = [lax.all_gather(w_down[layer, 0], "tensor") for layer in range(LAYERS)]
    route_rows = routes.reshape(LAYERS, plan.images, SEQ, 2)
    route_rows = jnp.pad(
        route_rows, ((0, 0), (0, 0), (0, PAD - SEQ), (0, 0)), constant_values=-1
    ).reshape(LAYERS, plan.rows, 2)
    route_rows = jnp.pad(
        route_rows, ((0, 0), (0, plan.lanes - plan.rows), (0, 0)), constant_values=-1
    ).transpose(0, 2, 1)
    router_rows = w_router.transpose(0, 2, 1)

    stream = pad_rows(tokens)
    kept = []
    for layer in range(LAYERS):
        after, *saved_one = attention_forward(
            stream, ln_gain[layer], ln_bias[layer], w_qkv[layer], w_out[layer], 4 * layer
        )
        following, *saved_two = moe_forward(
            plan, after, route_rows[layer], ln_gain[layer], ln_bias[layer], router_rows[layer],
            up_all[layer], down_all[layer], 4 * layer + 1,
        )
        kept.append((stream, after, saved_one, saved_two))
        stream = following
    result = cut_rows(stream).astype(BF16)
    grad = pad_rows(cotangent)
    per_layer = [None] * LAYERS
    for layer in reversed(range(LAYERS)):
        stream, after, saved_one, saved_two = kept[layer]
        grad, gup, gdown, grouter, gvec_two = moe_backward(
            plan, grad, after, saved_two, ln_gain[layer], router_rows[layer],
            up_all[layer], down_all[layer], 4 * layer + 2,
        )
        gup = lax.psum_scatter(gup, "tensor", scatter_dimension=0, tiled=False)
        gdown = lax.psum_scatter(gdown, "tensor", scatter_dimension=0, tiled=False)
        grad, gqkv, gout, gvec_one = attention_backward(
            grad, stream, saved_one, ln_gain[layer], w_qkv[layer], w_out[layer], 4 * layer + 3
        )
        grouter = lax.psum(grouter, ("expert", "tensor"))
        gqkv, gout, gvec = lax.psum(
            (gqkv, gout, jnp.stack([gvec_one[:2], gvec_two[:2]])), "expert"
        )
        gqkv = gqkv.reshape(512, 3, 128).transpose(1, 0, 2)
        per_layer[layer] = (
            gvec[:, 0], gvec[0, 1], gvec[1, 1], gqkv, gout, grouter.T,
            gup.astype(F32)[None], gdown.astype(F32)[None],
        )
    stacked = [jnp.stack([entry[member] for entry in per_layer]) for member in range(8)]
    return (result, cut_rows(grad), *stacked)


def solution(mesh):
    in_specs = (
        P("expert", None),
        P(None, "expert", None),
        P(),
        P(),
        P(None, None, None, "tensor"),
        P(None, "tensor", None),
        P(),
        P(None, "expert", None, "tensor"),
        P(None, "expert", "tensor", None),
        P("expert", None),
    )
    out_specs = (
        P("expert", None),
        P("expert", None),
        P(),
        P(),
        P(),
        P(None, None, None, "tensor"),
        P(None, "tensor", None),
        P(),
        P(None, "expert", None, "tensor"),
        P(None, "expert", "tensor", None),
    )
    return jax.shard_map(body, mesh=mesh, in_specs=in_specs, out_specs=out_specs, check_vma=False)
```

time: 1240 us -> 646 us (0.52)
  Pallas kernels: 0 us -> 331 us
  waiting for transfers between devices: 456 us -> 168 us
  local copies, waits for them, and re-layouts: 307 us -> 31.7 us
  blocking collectives: 225 us -> 79.4 us
  other arithmetic: 119 us -> 11.6 us
  matrix products: 86.4 us -> 0 us
  starting transfers between devices: 24.3 us -> 0.35 us
    pallas_call x0 -> x8, Pallas kernels: none -> 331 us  [the longest x2 122 us: moe_forward(): pl.pallas_call(kernel, name='moe_forward', out_shape=(jax.ShapeDtypeStruc...]
    all_to_all x3 -> x0, blocking collectives: 185 us -> none  [to_experts(): lax.all_to_all(slot_rows, 'expert', split_axis=1, concat_axis=1, tiled=True)]
    gather x24 -> x0, local copies, waits for them, and re-layouts: 155 us -> none  [the longest x10 39.2 us: layer_forward(): chosen = jnp.take_along_axis(logits, route_pair, 1)]
    all_to_all x5 -> x0, waiting for transfers between devices: 150 us -> none  [the longest x4 94.8 us: return_rows(): lax.all_to_all(whole_rows, 'expert', split_axis=1, concat_axis=1, tiled=T...]
    psum x5 -> x1, waiting for transfers between devices: 135 us -> 17.3 us  [body(): lax.psum((gqkv, gout, jnp.stack([gvec_one[:2], gvec_two[:2]])), 'expert')]
    dot_general x40 -> x0, matrix products: 82.4 us -> none  [the longest x2 17.9 us: layer_backward(): jnp.einsum('sd,fd->sf', recv_grad, down_local, preferred_element_type=jnp...]
    reduce_sum x21 -> x0, other arithmetic: 77 us -> none  [the longest x2 40.9 us: layer_backward(): gate_grad = jnp.sum(grad_stream[:, None, :] * saved['picked'], -1)]
    all_gather x4, waiting for transfers between devices: 79.3 us -> 18.4 us  [the longest x2 18.4 us: body(): lax.all_gather(w_down[layer, 0], 'tensor')]
  transfers between devices with their start and end apart: 18 -> 9, of which waited for: 16 -> 6; matrix products, arithmetic and copies ran while one was open for 18% -> 3% of each run, Pallas kernels for 0% -> 17%
where the time goes in v1:
time: 646 us; the launch traced here: 637 us
  Pallas kernels  331 us (51%)
  waiting for transfers between devices  168 us (26%)
  blocking collectives  79.4 us (12%)
  local copies, waits for them, and re-layouts  31.7 us (5%)
  between operations  14.8 us (2%)
  other arithmetic  11.6 us (2%)
    pallas_call x2, Pallas kernels, moe_forward(): pl.pallas_call(kernel, name='moe_forward', out_shape=(jax.ShapeDtypeStruc...  122 us
    pallas_call x2, Pallas kernels, moe_backward(): pl.pallas_call(kernel, name='moe_backward', out_shape=(jax.ShapeDtypeStru...  121 us
    reduce_scatter x2, waiting for transfers between devices, body(): gdown = lax.psum_scatter(gdown, 'tensor', scatter_dimension=0, tiled=False)  65.5 us
    reduce_scatter x2, waiting for transfers between devices, body(): gup = lax.psum_scatter(gup, 'tensor', scatter_dimension=0, tiled=False)  63.1 us
    pallas_call x2, Pallas kernels, attention_forward(): pl.pallas_call(kernel, name='attention_forward', out_shape=(jax.ShapeDtyp...  46 us
    pallas_call x2, Pallas kernels, attention_backward(): pl.pallas_call(kernel, name='attention_backward', out_shape=(jax.ShapeDty...  42.1 us
    psum x1, blocking collectives, body(): lax.psum((gqkv, gout, jnp.stack([gvec_one[:2], gvec_two[:2]])), 'expert')  42.1 us
    psum x1, blocking collectives, body(): grouter = lax.psum(grouter, ('expert', 'tensor'))  37.4 us
  transfers between devices with their start and end apart: 9, of which 6 were waited for; matrix products, arithmetic and copies ran while one was open for 3% of the time, Pallas kernels for 17%

profile of v1, /device:TPU:0, one launch (start us, length us, event | category | flops | bytes accessed | tf_op | source)
XLA Modules:
  0.0 636.7 jit_solution(1301700889655326505)
XLA Ops:
  7.2 2.3 fusion.1
  9.6 1.0 fusion
  10.8 0.7 all-gather.13.cloned.1.call-update
  14.6 29.1 %attention_forward.2 = (f32[1040,512]{1,0:T(8,128)S(1)}, bf16[1040,512]{1,0:T(8,128)(2,1)S(1)}, bf16[1040,384]{1,0:T(8,128)(2,1)S(1)}, bf16[5,416,208]{2,1,0:T(8,128)(2,1)S(1)}, bf16[1040,128]{1,0:T(8,128)(2,1)S(1)}) custom-call(f32[1040,512]{1,0:T(8,128)S(1)} %bitcast_convert_fusion.1.refs_0_.refs_1_, ...), custom_call_target="tpu_custom_call" | custom-call | tf_op jit(solution)/shard_map/attention_forward/pallas_call | solution.py:293
  43.7 1.4 copy-done.1
  45.0 1.0 copy-done.4
  46.0 1.0 copy-done.6
  47.0 0.9 copy-done.8
  47.9 0.7 copy-done.13
  49.8 1.7 bitcast_convert_fusion.refs_0_
  51.5 18.4 %all-gather.11.cloned.1.call-done = bf16[4,1,512,512]{3,2,1,0:T(8,128)(2,1)} async-done(((bf16[1,1,512,512]{3,2,1,0:T(8,128)(2,1)}), bf16[4,1,512,512]{3,2,1,0:T(8,128)(2,1)}) %all-gather.11.cloned.1.call-update) | async-done | bytes 2097168 | tf_op jit(solution)/shard_map/all_gather | solution.py:690
  69.9 63.0 %moe_forward.2 = (f32[1040,512]{1,0:T(8,128)}, bf16[1152,512]{1,0:T(8,128)(2,1)}, bf16[640,512]{1,0:T(8,128)(2,1)}, bf16[640,512]{1,0:T(8,128)(2,1)}, f32[8,1152]{1,0:T(8,128)}, /*index=5*/f32[8,1152]{1,0:T(8,128)}) custom-call(f32[1040,512]{1,0:T(8,128)} %copy-done.1, s32[2,1152]{1,0:T(2,128)} %get-tuple-element.137.refs_1_, f32[2,512]{1,0:T(2,128)} %copy-done.17, ...), custom_call_target="tpu_custom_call" | custom-call | tf_op jit(solution)/shard_map/moe_forward/pallas_call | solution.py:525
  132.9 1.6 copy-done.2
  134.5 16.9 %attention_forward.3 = (f32[1040,512]{1,0:T(8,128)S(1)}, bf16[1040,512]{1,0:T(8,128)(2,1)S(1)}, bf16[1040,384]{1,0:T(8,128)(2,1)S(1)}, bf16[5,416,208]{2,1,0:T(8,128)(2,1)S(1)}, bf16[1040,128]{1,0:T(8,128)(2,1)S(1)}) custom-call(f32[1040,512]{1,0:T(8,128)S(1)} %copy-done.2, f32[2,512]{1,0:T(2,128)S(1)} %get-tuple-element.149.refs_1_.refs_2_.refs_7_.refs_6_, ...), custom_call_target="tpu_custom_call" | custom-call | tf_op jit(solution)/shard_map/attention_forward/pallas_call | solution.py:293
  151.4 1.3 copy-done.3
  152.7 0.9 copy-done.10
  153.6 59.0 %moe_forward.3 = (f32[1040,512]{1,0:T(8,128)}, bf16[1152,512]{1,0:T(8,128)(2,1)}, bf16[640,512]{1,0:T(8,128)(2,1)}, bf16[640,512]{1,0:T(8,128)(2,1)}, f32[8,1152]{1,0:T(8,128)}, /*index=5*/f32[8,1152]{1,0:T(8,128)}) custom-call(f32[1040,512]{1,0:T(8,128)} %copy-done.3, s32[2,1152]{1,0:T(2,128)} %get-tuple-element.136.refs_1_, f32[2,512]{1,0:T(2,128)} %copy-done.19, ...), custom_call_target="tpu_custom_call" | custom-call | tf_op jit(solution)/shard_map/moe_forward/pallas_call | solution.py:525
  212.7 60.0 %moe_backward.2 = (f32[1040,512]{1,0:T(8,128)}, bf16[4,512,512]{2,1,0:T(8,128)(2,1)}, bf16[4,512,512]{2,1,0:T(8,128)(2,1)}, f32[8,512]{1,0:T(8,128)}, f32[8,512]{1,0:T(8,128)}) custom-call(f32[1040,512]{1,0:T(8,128)} %bitcast_convert_fusion.refs_0_, f32[1040,512]{1,0:T(8,128)} %copy-done.3, bf16[1152,512]{1,0:T(8,128)(2,1)} %get-tuple-element.54.refs_2_, ...), custom_call_target="tpu_custom_call" | custom-call | tf_op jit(solution)/shard_map/moe_backward/pallas_call | solution.py:646
  272.7 1.1 copy-done.11
  273.8 21.2 %attention_backward.2 = (f32[1040,512]{1,0:T(8,128)}, f32[512,384]{1,0:T(8,128)S(1)}, f32[128,512]{1,0:T(8,128)S(1)}, f32[8,512]{1,0:T(8,128)S(1)}) custom-call(f32[1040,512]{1,0:T(8,128)} %get-tuple-element.59.refs_0_, f32[1040,512]{1,0:T(8,128)} %get-tuple-element.51.refs_0_.refs_1_, bf16[1040,512]{1,0:T(8,128)(2,1)S(1)} %get-tuple-element.60.refs_2_, ...), custom_call_target="tpu_custom_call" | custom-call | tf_op jit(solution)/shard_map/attention_backward/pallas_call | solution.py:381
  295.0 0.9 copy-done.12
  295.9 0.7 copy-done.15
  296.6 2.3 copy.36
  298.9 60.7 %moe_backward.3 = (f32[1040,512]{1,0:T(8,128)}, bf16[4,512,512]{2,1,0:T(8,128)(2,1)}, bf16[4,512,512]{2,1,0:T(8,128)(2,1)}, f32[8,512]{1,0:T(8,128)}, f32[8,512]{1,0:T(8,128)}) custom-call(f32[1040,512]{1,0:T(8,128)} %get-tuple-element.64.refs_0_, f32[1040,512]{1,0:T(8,128)} %copy-done.1, bf16[1152,512]{1,0:T(8,128)(2,1)} %get-tuple-element.65.refs_2_, ...), custom_call_target="tpu_custom_call" | custom-call | tf_op jit(solution)/shard_map/moe_backward/pallas_call | solution.py:646
  359.6 1.1 copy-done.9
  360.7 20.9 %attention_backward.3 = (f32[1040,512]{1,0:T(8,128)}, f32[512,384]{1,0:T(8,128)S(1)}, f32[128,512]{1,0:T(8,128)S(1)}, f32[8,512]{1,0:T(8,128)S(1)}) custom-call(f32[1040,512]{1,0:T(8,128)} %get-tuple-element.70.refs_0_, f32[1040,512]{1,0:T(8,128)} %copy-done, bf16[1040,512]{1,0:T(8,128)(2,1)S(1)} %copy-done.5, bf16[1040,384]{1,0:T(8,128)(2,1)S(1)} %copy-done.9, ...), custom_call_target="tpu_custom_call" | custom-call | tf_op jit(solution)/shard_map/attention_backward/pallas_call | solution.py:381
  381.6 0.7 copy-done.16
  382.3 1.1 copy.35
  384.1 0.7 reduce-scatter.5.cloned.1.call-update
  384.9 0.7 reduce-scatter.11.cloned.1.call-update
  385.6 0.7 reduce-scatter.9.cloned.1.call-update
  386.7 1.2 convert_element_type.53
  387.9 1.7 slice.132
  389.7 1.5 reshape.120
  391.2 0.7 slice_bitcast_fusion.10
  392.0 0.7 slice_bitcast_fusion.12
  392.7 42.1 %all-reduce.5 = (f32[2,2,512]{2,1,0:T(2,128)S(1)}, f32[2,2,512]{2,1,0:T(2,128)S(1)}) all-reduce(f32[2,2,512]{2,1,0:T(2,128)S(1)} %pad_maximum_fusion.4, f32[2,2,512]{2,1,0:T(2,128)S(1)} %pad_maximum_fusion.3), channel_id=1, replica_groups=mesh['expert'=8,'tensor'=4] {'expert'}, use_global_device_ids=true, to_apply=%region_1.2 | all-reduce | flops 4096 | bytes 32768 | tf_op jit(solution)/shard_map/psum | solution.py:727
  435.4 37.4 %all-reduce.4 = (f32[1,512,8]{1,2,0:T(8,128)S(1)}, f32[1,512,8]{1,2,0:T(8,128)S(1)}) all-reduce(f32[1,512,8]{1,2,0:T(8,128)S(1)} %bitcast.104, f32[1,512,8]{1,2,0:T(8,128)S(1)} %bitcast.105), channel_id=1, replica_groups=mesh['expert'=8,'tensor'=4] {'expert','tensor'}, use_global_device_ids=true, to_apply=%region_7.8 | all-reduce | flops 8192 | bytes 65536 | tf_op jit(solution)/shard_map/psum | solution.py:726
  474.6 17.3 %all-reduce.9.cloned.1.call-done = (f32[1,3,512,128]{2,3,1,0:T(8,128)}, f32[1,3,512,128]{2,3,1,0:T(8,128)}, f32[1,128,512]{2,1,0:T(8,128)}, f32[1,128,512]{2,1,0:T(8,128)}) async-done(((f32[1,3,512,128]{2,3,1,0:T(8,128)}, f32[1,3,512,128]{2,3,1,0:T(8,128)}, f32[1,128,512]{2,1,0:T(8,128)}, f32[1,128,512]{2,1,0:T(8,128)}), (f32[1,3,512,128]{2,3,1,0:T(8,128)}, f32[1,3,512,128]{2,3,1,0:T(8,128)}, ...) | async-done | bytes 2097168 | tf_op jit(solution)/shard_map/psum | solution.py:727
  491.9 1.5 pad_maximum_fusion
  493.4 1.6 copy.38
  495.0 0.8 pad_maximum_fusion.1
  495.8 28.9 %reduce-scatter.7.cloned.1.call-done = bf16[1,512,512]{2,1,0:T(8,128)(2,1)} async-done(((bf16[4,512,512]{2,1,0:T(8,128)(2,1)}), bf16[1,512,512]{2,1,0:T(8,128)(2,1)}) %reduce-scatter.7.cloned.1.call-update) | async-done | bytes 524304 | tf_op jit(solution)/shard_map/reduce_scatter | solution.py:721
  524.8 34.1 %reduce-scatter.5.cloned.1.call-done = bf16[1,512,512]{2,1,0:T(8,128)(2,1)} async-done(((bf16[4,512,512]{2,1,0:T(8,128)(2,1)}), bf16[1,512,512]{2,1,0:T(8,128)(2,1)}) %reduce-scatter.5.cloned.1.call-update) | async-done | bytes 524304 | tf_op jit(solution)/shard_map/reduce_scatter | solution.py:721
  558.9 2.7 maximum_convert_fusion
  561.6 31.4 %reduce-scatter.11.cloned.1.call-done = bf16[1,512,512]{2,1,0:T(8,128)(2,1)} async-done(((bf16[4,512,512]{2,1,0:T(8,128)(2,1)}), bf16[1,512,512]{2,1,0:T(8,128)(2,1)}) %reduce-scatter.11.cloned.1.call-update) | async-done | bytes 524304 | tf_op jit(solution)/shard_map/reduce_scatter | solution.py:722
  592.9 34.2 %reduce-scatter.9.cloned.1.call-done = bf16[1,512,512]{2,1,0:T(8,128)(2,1)} async-done(((bf16[4,512,512]{2,1,0:T(8,128)(2,1)}), bf16[1,512,512]{2,1,0:T(8,128)(2,1)}) %reduce-scatter.9.cloned.1.call-update) | async-done | bytes 524304 | tf_op jit(solution)/shard_map/reduce_scatter | solution.py:722
  627.1 2.7 maximum_convert_fusion.1
  (107 shorter events, 8.0 us)
Async XLA Ops:
  7.2 2.4 copy-start.24
  7.2 44.3 %all-gather.9.cloned.1.call-start = ((), (), s32[]{:S(2)}) async-start(), calls=%async_computation.8 | async-start | bytes 2621440 | tf_op jit(solution)/shard_map/all_gather | solution.py:689
  9.5 2.5 copy-start.25
  9.6 60.3 %all-gather.11.cloned.1.call-start = ((), (), s32[]{:S(2)}) async-start(), calls=%async_computation.9 | async-start | bytes 2621440 | tf_op jit(solution)/shard_map/all_gather | solution.py:690
  10.7 1.7 copy-start.31
  10.7 1.9 copy-start.26
  10.7 142.9 %all-gather.13.cloned.1.call-start = ((), (), s32[]{:S(2)}) async-start(), calls=%async_computation.10 | async-start | bytes 2621440 | tf_op jit(solution)/shard_map/all_gather | solution.py:689
  11.4 142.2 %all-gather.15.cloned.1.call-start = ((), (), s32[]{:S(2)}) async-start(), calls=%async_computation.11 | async-start | bytes 2621440 | tf_op jit(solution)/shard_map/all_gather | solution.py:690
  12.0 479.9 %all-reduce.9.cloned.1.call-start = ((), (), s32[]{:S(2)}) async-start(), calls=%async_computation.12 | async-start | bytes 4194304 | tf_op jit(solution)/shard_map/psum | solution.py:727
  12.9 0.7 copy-start.35
  12.9 0.7 copy-start.36
  12.9 1.0 copy-start.28
  12.9 1.2 copy-start.27
  13.9 0.7 copy-start.17
  13.9 0.7 copy-start.22
  13.9 119.0 %copy-start.19 = (f32[2,512]{1,0:T(2,128)}, f32[2,512]{1,0:T(2,128)S(1)}, u32[]{:S(2)}) copy-start(f32[2,512]{1,0:T(2,128)S(1)} %get-tuple-element.149.refs_1_.refs_2_.refs_7_.refs_6_) | copy-start | bytes 12292
  13.9 119.0 %copy-start.21 = (f32[2,512]{1,0:T(2,128)}, f32[2,512]{1,0:T(2,128)S(1)}, u32[]{:S(2)}) copy-start(f32[2,512]{1,0:T(2,128)S(1)} %get-tuple-element.144.refs_2_.refs_3_) | copy-start | bytes 12292
  14.5 36.9 %copy-start = (f32[1040,512]{1,0:T(8,128)}, f32[1040,512]{1,0:T(8,128)S(1)}, u32[]{:S(2)}) copy-start(f32[1040,512]{1,0:T(8,128)S(1)} %bitcast_convert_fusion.1.refs_0_.refs_1_) | copy-start | bytes 6389764
  14.6 34.0 %copy-start.32 = (bf16[2,512,8]{1,2,0:T(8,128)(2,1)S(1)}, bf16[2,512,8]{1,2,0:T(8,128)(2,1)}, u32[]{:S(2)}) copy-start(bf16[2,512,8]{1,2,0:T(8,128)(2,1)} %param.16) | copy-start | bytes 49156
  43.7 1.4 copy-start.1
  45.0 1.0 copy-start.4
  46.0 1.0 copy-start.6
  47.0 0.9 copy-start.8
  47.9 0.7 copy-start.13
  132.9 1.6 copy-start.2
  151.4 1.3 copy-start.3
  152.7 0.9 copy-start.10
  212.7 60.0 %copy-start.20 = (f32[2,512]{1,0:T(2,128)S(1)}, f32[2,512]{1,0:T(2,128)}, u32[]{:S(2)}) copy-start(f32[2,512]{1,0:T(2,128)} %copy-done.19) | copy-start | bytes 12292
  272.7 1.1 copy-start.11
  295.0 0.9 copy-start.12
  295.9 0.7 copy-start.15
  298.9 60.7 %copy-start.5 = (bf16[1040,512]{1,0:T(8,128)(2,1)S(1)}, bf16[1040,512]{1,0:T(8,128)(2,1)}, u32[]{:S(2)}) copy-start(bf16[1040,512]{1,0:T(8,128)(2,1)} %copy-done.4) | copy-start | bytes 3194884
  298.9 60.7 %copy-start.7 = (bf16[5,416,208]{2,1,0:T(8,128)(2,1)S(1)}, bf16[5,416,208]{2,1,0:T(8,128)(2,1)}, u32[]{:S(2)}) copy-start(bf16[5,416,208]{2,1,0:T(8,128)(2,1)} %copy-done.6) | copy-start | bytes 2595844
  298.9 60.7 %copy-start.14 = (bf16[1040,128]{1,0:T(8,128)(2,1)S(1)}, bf16[1040,128]{1,0:T(8,128)(2,1)}, u32[]{:S(2)}) copy-start(bf16[1040,128]{1,0:T(8,128)(2,1)} %copy-done.13) | copy-start | bytes 798724
  298.9 60.7 %copy-start.18 = (f32[2,512]{1,0:T(2,128)S(1)}, f32[2,512]{1,0:T(2,128)}, u32[]{:S(2)}) copy-start(f32[2,512]{1,0:T(2,128)} %copy-done.17) | copy-start | bytes 12292
  359.6 1.1 copy-start.9
  381.6 0.7 copy-start.16
  383.5 141.3 %reduce-scatter.7.cloned.1.call-start = ((), (), s32[]{:S(2)}) async-start(), calls=%async_computation.5 | async-start | bytes 2621440 | tf_op jit(solution)/shard_map/reduce_scatter | solution.py:721
  384.1 174.8 %reduce-scatter.5.cloned.1.call-start = ((), (), s32[]{:S(2)}) async-start(), calls=%async_computation.4 | async-start | bytes 2621440 | tf_op jit(solution)/shard_map/reduce_scatter | solution.py:721
  384.8 208.1 %reduce-scatter.11.cloned.1.call-start = ((), (), s32[]{:S(2)}) async-start(), calls=%async_computation.7 | async-start | bytes 2621440 | tf_op jit(solution)/shard_map/reduce_scatter | solution.py:722
  384.9 1.6 copy-start.23
  385.6 241.5 %reduce-scatter.9.cloned.1.call-start = ((), (), s32[]{:S(2)}) async-start(), calls=%async_computation.6 | async-start | bytes 2621440 | tf_op jit(solution)/shard_map/reduce_scatter | solution.py:722
  389.7 45.7 %copy-start.33 = (f32[8,512]{1,0:T(8,128)S(1)}, f32[8,512]{1,0:T(8,128)}, u32[]{:S(2)}) copy-start(f32[8,512]{1,0:T(8,128)} %get-tuple-element.85) | copy-start | bytes 49156
  389.7 45.7 %copy-start.34 = (f32[8,512]{1,0:T(8,128)S(1)}, f32[8,512]{1,0:T(8,128)}, u32[]{:S(2)}) copy-start(f32[8,512]{1,0:T(8,128)} %get-tuple-element.84) | copy-start | bytes 49156
  493.4 1.6 copy-start.29
  493.4 1.6 copy-start.30
Sparse Core Ops, SparseCore 0:
  10.2 34.8 all-gather.8
  46.7 23.1 all-gather.10
  72.0 22.5 all-gather.12
  96.6 28.0 all-gather.14
  383.6 108.2 all-reduce.8
  494.3 30.4 reduce-scatter.6
  527.5 31.3 reduce-scatter.4
  561.4 31.4 reduce-scatter.10
  595.6 31.4 reduce-scatter.8
